TPU v7x, 32 devices: a whole 2x2x4 slice. The times are simulated.
32 devices in a mesh: seq: 4 (over z), tp: 8 (over y, x, core).
Axes of the slice: x: 2, y: 2, z: 4, core: 2. Of those that a mesh axis runs over, the one named last changes fastest.
Arguments:
- residual: bfloat16 [8192, 2048], P('seq', 'tp'), may hold values from -6 to 6
- attn_gain: bfloat16 [2048], replicated, may hold values from 0.25 to 1.75
- attn_in: bfloat16 [3, 2048, 2048], P(None, None, 'tp')
- attn_out: bfloat16 [2048, 2048], P('tp'), may hold values from -0.125 to 0.125
- ffn_gain: bfloat16 [2048], replicated, may hold values from 0.25 to 1.75
- ffn_in: bfloat16 [2, 2048, 20480], P(None, None, 'tp'), may hold values from -0.125 to 0.125
- ffn_out: bfloat16 [20480, 2048], P('tp'), may hold values from -0.0390625 to 0.0390625
- route_rows: int32 [4, 224], P('seq'), may hold values from 0 to 2047, as said below
- route_counts: int32 [4], replicated, may hold values from 1 to 224, 512 in all
Outputs:
- layer_out: bfloat16 [8192, 2048], P('seq', 'tp')
Inputs may be any that keep to these rules, and one draw needn't show every extreme that they name: `route_rows`: in each row s the 224 entries are distinct positions of that shard; only the first route_counts[s] entries are used; each row holds 0 and 2047. `route_counts`: the counts sum to 512 and the largest is exactly 224.
All inputs are finite; a program needn't handle non-finite values.
Results may differ from a plain program's by a relative error of at most 0.014.
Values may be sent and summed in bfloat16 or wider, within the bound.
No kernel may reach another device: no remote copies, remote signals or barrier semaphores. Data moves between devices by JAX's collectives and lax.ppermute only.
A program may use at most 128 MiB of HBM per device.

v0:
```python
import jax
import jax.numpy as jnp
from jax import lax
from jax.sharding import PartitionSpec as P

HD = 64
RADIUS = 127


epsilon = 1e-06


def extended(block, sides, width):
    for axis, dim in sides:
        count = lax.axis_size(axis)
        forward = [(i, i + 1) for i in range(count - 1)]
        backward = [(target, source) for source, target in forward]
        low = lax.ppermute(
            lax.slice_in_dim(block, block.shape[dim] - width, None, axis=dim), axis, forward
        )
        high = lax.ppermute(lax.slice_in_dim(block, 0, width, axis=dim), axis, backward)
        block = jnp.concatenate([low, block, high], axis=dim)
    return block


def rms_norm(values, gain_row):
    wide = values.astype(jnp.float32)
    mean_square = jnp.mean(wide * wide, axis=-1, keepdims=True)
    return (wide * lax.rsqrt(mean_square + epsilon) * gain_row.astype(jnp.float32)).astype(
        jnp.bfloat16
    )


def heavy_branch(rows_part, ffn_gain, ffn_in, ffn_out):
    full_rows = lax.all_gather(rows_part, "tp", axis=1, tiled=True)
    normed_rows = rms_norm(full_rows, ffn_gain)
    both = jnp.einsum("nd,kdf->knf", normed_rows, ffn_in, preferred_element_type=jnp.float32)
    hidden = (jax.nn.gelu(both[0], approximate=True) * both[1]).astype(jnp.bfloat16)
    partial_value = jnp.dot(hidden, ffn_out, preferred_element_type=jnp.float32)
    return lax.psum_scatter(
        partial_value.astype(jnp.bfloat16), "tp", scatter_dimension=1, tiled=True
    ).astype(jnp.float32)


def local(
    residual, attn_gain, attn_in, attn_out, ffn_gain, ffn_in, ffn_out, route_rows, route_counts
):
    seq_count = lax.axis_size("seq")
    seq_index = lax.axis_index("seq")
    whole = lax.all_gather(residual, "tp", axis=1, tiled=True)
    tok_rows = whole.shape[0]
    normed = rms_norm(whole, attn_gain)
    projected = jnp.einsum(
        "td,kdh->kth", normed, attn_in, preferred_element_type=jnp.float32
    ).astype(jnp.bfloat16)
    local_width = projected.shape[2]
    local_heads = local_width // HD
    paired = jnp.concatenate([projected[1], projected[2]], axis=1)
    padded = extended(paired, (("seq", 0),), RADIUS)
    block = min(512, tok_rows)
    span = block + 2 * RADIUS
    queries_all = projected[0]

    def attend(block_id):
        start = block_id * block
        query_blk = lax.dynamic_slice_in_dim(queries_all, start, block, 0).reshape(
            block, local_heads, HD
        )
        both_blk = lax.dynamic_slice_in_dim(padded, start, span, 0)
        key_blk = both_blk[:, :local_width].reshape(span, local_heads, HD)
        value_blk = both_blk[:, local_width:].reshape(span, local_heads, HD)
        query_pos = seq_index * tok_rows + start + jnp.arange(block, dtype=jnp.int32)
        key_pos = seq_index * tok_rows + start - RADIUS + jnp.arange(span, dtype=jnp.int32)
        usable = (
            (jnp.abs(query_pos[:, None] - key_pos[None, :]) <= RADIUS)
            & (key_pos[None, :] >= 0)
            & (key_pos[None, :] < seq_count * tok_rows)
        )
        scores = (
            jnp.einsum("qhd,khd->hqk", query_blk, key_blk, preferred_element_type=jnp.float32)
            / HD**0.5
        )
        scores = jnp.where(usable[None], scores, -jnp.inf)
        top = jnp.max(scores, axis=-1, keepdims=True)
        expo = jnp.exp(scores - top)
        prob_rows = (expo / jnp.sum(expo, axis=-1, keepdims=True)).astype(jnp.bfloat16)
        context_blk = jnp.einsum(
            "hqk,khd->qhd", prob_rows, value_blk, preferred_element_type=jnp.float32
        )
        return context_blk.astype(jnp.bfloat16).reshape(block, local_width)

    context = lax.map(attend, jnp.arange(tok_rows // block, dtype=jnp.int32)).reshape(
        tok_rows, local_width
    )
    grouped = lax.all_to_all(context, "tp", split_axis=0, concat_axis=1, tiled=True)
    mixed_rows = jnp.dot(
        grouped,
        lax.all_gather(attn_out, "tp", axis=0, tiled=True),
        preferred_element_type=jnp.float32,
    )
    mixed = lax.all_to_all(
        mixed_rows.astype(jnp.bfloat16), "tp", split_axis=1, concat_axis=0, tiled=True
    ).astype(mixed_rows.dtype)
    updated = (residual.astype(jnp.float32) + mixed).astype(jnp.bfloat16)
    slot_total = route_rows.shape[1]
    slots = jnp.arange(slot_total, dtype=jnp.int32)
    row_index = route_rows[0]
    row_count = lax.dynamic_index_in_dim(route_counts, seq_index, 0, keepdims=False)
    usable_slots = slots < row_count
    taken = jnp.take(updated, row_index, axis=0)
    heavy = heavy_branch(taken, ffn_gain, ffn_in, ffn_out)
    heavy = jnp.where(usable_slots[:, None], heavy, 0.0)
    result = updated.astype(jnp.float32).at[row_index].add(heavy)
    return result.astype(jnp.bfloat16)


def solution(mesh):
    in_specs = (
        P("seq", "tp"),
        P(),
        P(None, None, "tp"),
        P("tp", None),
        P(),
        P(None, None, "tp"),
        P("tp", None),
        P("seq", None),
        P(),
    )
    out_specs = P("seq", "tp")
    return jax.shard_map(local, mesh=mesh, in_specs=in_specs, out_specs=out_specs, check_vma=False)
```

profile of v0, /device:TPU:0, one launch (start us, length us, event | category | flops | bytes accessed | tf_op | source)
XLA Modules:
  0.0 284.9 jit_solution(11498407260636012959)
XLA Ops:
  6.5 0.7 all-gather.3.cloned.1.call-update
  7.3 0.7 all-gather.5.cloned.1.call-update
  8.0 0.7 convert_element_type.74
  8.7 59.2 %all-gather.3.cloned.1.call-done = bf16[2048,2048]{1,0:T(8,128)(2,1)} async-done(((bf16[2048,256]{1,0:T(8,128)(2,1)}), bf16[2048,2048]{1,0:T(8,128)(2,1)}) %all-gather.3.cloned.1.call-update) | async-done | bytes 8388624 | tf_op jit(solution)/shard_map/all_gather | solution.py:50
  67.9 5.2 %fusion.15 = f32[2048]{0:T(1024)S(1)} fusion(bf16[2048,2048]{1,0:T(8,128)(2,1)} %all-gather.3.cloned.1.call-done), kind=kLoop, calls=%fused_computation.27 | loop fusion | flops 12580864 | bytes 8396800 | tf_op jit(solution)/shard_map/reduce_sum | solution.py:28
  73.2 0.5 copy-done.2
  73.7 7.7 %fusion.26 = bf16[3,2048,256]{1,2,0:T(8,128)(2,1)S(1)} fusion(bf16[3,2048,256]{2,1,0:T(8,128)(2,1)S(1)} %copy-done, bf16[2048,2048]{1,0:T(8,128)(2,1)S(1)} %copy-done.2, f32[2048]{0:T(1024)S(1)} %convert_element_type.74, f32[2048]{0:T(1024)S(1)} %add_rsqrt_fusion), kind=kOutput, calls=%fused_computation.37 | convolution fusion | flops 6460801024 | bytes 14696448 | tf_op jit(solution)/shard_map/td,kdh->kth/dot_general | solution.py:53
  81.4 1.2 slice_bitcast_fusion.2
  82.7 3.4 %collective-permute-start = (bf16[127,512]{0,1:T(8,128)(2,1)S(1)}, bf16[127,512]{0,1:T(8,128)(2,1)S(1)}, u32[]{:S(2)}, u32[]{:S(2)}) collective-permute-start(bf16[127,512]{0,1:T(8,128)(2,1)S(1)} %get-tuple-element.109), channel_id=1, source_target_pairs={{0,8},{8,16},{16,24},{1,9},{9,17},{17,25},{2,10},{10,18},{18,26},{... | collective-permute-start | bytes 390152 | tf_op jit(solution)/shard_map/ppermute | solution.py:18
  86.1 1.3 collective-permute-start.1
  87.4 1.6 pad_maximum_fusion
  89.0 0.2 collective-permute-done
  89.3 4.1 %collective-permute-done.1 = bf16[127,512]{0,1:T(8,128)(2,1)S(1)} collective-permute-done((bf16[127,512]{0,1:T(8,128)(2,1)S(1)}, bf16[127,512]{0,1:T(8,128)(2,1)S(1)}, u32[]{:S(2)}, u32[]{:S(2)}) %collective-permute-start.1) | collective-permute-done | bytes 130080 | tf_op jit(solution)/shard_map/ppermute | solution.py:21
  93.4 4.5 %concatenate.7 = bf16[2302,512]{0,1:T(8,128)(2,1)S(1)} concatenate(bf16[127,512]{0,1:T(8,128)(2,1)S(1)} %collective-permute-done, bf16[2048,512]{0,1:T(8,128)(2,1)} %pad_maximum_fusion, bf16[127,512]{0,1:T(8,128)(2,1)S(1)} %collective-permute-done.1), dimensions={0} | concatenate | bytes 4714496 | tf_op jit(solution)/shard_map/concatenate | solution.py:22
  97.9 59.3 %while.12 = (s32[]{:T(128)}, bf16[4,512,256]{2,1,0:T(8,128)(2,1)}, s32[4]{0:T(128)S(1)}, bf16[2302,512]{0,1:T(8,128)(2,1)S(1)}, s32[]{:T(128)}, /*index=5*/bf16[...) while((s32[]{:T(128)}, bf16[4,512,256]{2,1,0:T(8,128)(2,1)}, ...), condition=%wide.region_4.5_spmd, body=%wide.region_1.4_spmd.sunk | while | flops 413113600 | bytes 17815284 | solution.py:92
  97.9 0.6 dynamic_slice.28
  99.2 0.6 fusion.86
  99.8 0.4 constant_dynamic-slice_fusion.4
  100.2 1.7 constant_dynamic-slice_fusion.5
  101.9 6.0 %fusion.87 = (f32[4,512]{1,0:T(4,128)S(1)}, f32[4,512,766]{2,1,0:T(8,128)}) fusion(pred[512,766]{1,0:T(8,128)(4,1)S(1)} %fusion.86, bf16[512,4,64]{0,2,1:T(8,128)(2,1)} %bitcast.85, bf16[766,4,64]{0,2,1:T(8,128)(2,1)S(1)} %bitcast.83), kind=kOutput, calls=%fused_computation.94.clone.1 | convolution fusion | flops 207078144 | bytes 7329792 | tf_op jit(solution)/shard_map/while/body/eval_jaxpr/sub | solution.py:85
  107.9 4.0 %fusion.88 = bf16[4,64,512]{2,1,0:T(8,128)(2,1)S(1)} fusion(bf16[766,4,64]{0,2,1:T(8,128)(2,1)S(1)} %bitcast.82, f32[4,512,766]{2,1,0:T(8,128)} %get-tuple-element.157, f32[4,512]{1,0:T(4,128)S(1)} %get-tuple-element.158), kind=kOutput, calls=%fused_computation.14.clone.1 | convolution fusion | flops 204070912 | bytes 6937600 | tf_op jit(solution)/shard_map/while/body/eval_jaxpr/hqk,khd->qhd/dot_general | solution.py:87
  111.9 0.1 copy.27
  112.0 0.7 constant_dynamic-update-slice_fusion.2
  112.8 0.6 dynamic_slice.28
  114.0 0.6 fusion.86
  114.6 0.4 constant_dynamic-slice_fusion.4
  115.1 1.7 constant_dynamic-slice_fusion.5
  116.7 6.0 %fusion.87 = (f32[4,512]{1,0:T(4,128)S(1)}, f32[4,512,766]{2,1,0:T(8,128)}) fusion(pred[512,766]{1,0:T(8,128)(4,1)S(1)} %fusion.86, bf16[512,4,64]{0,2,1:T(8,128)(2,1)} %bitcast.85, bf16[766,4,64]{0,2,1:T(8,128)(2,1)S(1)} %bitcast.83), kind=kOutput, calls=%fused_computation.94.clone.1 | convolution fusion | flops 207078144 | bytes 7329792 | tf_op jit(solution)/shard_map/while/body/eval_jaxpr/sub | solution.py:85
  122.8 4.0 %fusion.88 = bf16[4,64,512]{2,1,0:T(8,128)(2,1)S(1)} fusion(bf16[766,4,64]{0,2,1:T(8,128)(2,1)S(1)} %bitcast.82, f32[4,512,766]{2,1,0:T(8,128)} %get-tuple-element.157, f32[4,512]{1,0:T(4,128)S(1)} %get-tuple-element.158), kind=kOutput, calls=%fused_computation.14.clone.1 | convolution fusion | flops 204070912 | bytes 6937600 | tf_op jit(solution)/shard_map/while/body/eval_jaxpr/hqk,khd->qhd/dot_general | solution.py:87
  126.8 0.1 copy.27
  126.9 0.7 constant_dynamic-update-slice_fusion.2
  127.6 0.6 dynamic_slice.28
  128.9 0.6 fusion.86
  129.5 0.4 constant_dynamic-slice_fusion.4
  129.9 1.7 constant_dynamic-slice_fusion.5
  131.6 6.0 %fusion.87 = (f32[4,512]{1,0:T(4,128)S(1)}, f32[4,512,766]{2,1,0:T(8,128)}) fusion(pred[512,766]{1,0:T(8,128)(4,1)S(1)} %fusion.86, bf16[512,4,64]{0,2,1:T(8,128)(2,1)} %bitcast.85, bf16[766,4,64]{0,2,1:T(8,128)(2,1)S(1)} %bitcast.83), kind=kOutput, calls=%fused_computation.94.clone.1 | convolution fusion | flops 207078144 | bytes 7329792 | tf_op jit(solution)/shard_map/while/body/eval_jaxpr/sub | solution.py:85
  137.6 3.9 %fusion.88 = bf16[4,64,512]{2,1,0:T(8,128)(2,1)S(1)} fusion(bf16[766,4,64]{0,2,1:T(8,128)(2,1)S(1)} %bitcast.82, f32[4,512,766]{2,1,0:T(8,128)} %get-tuple-element.157, f32[4,512]{1,0:T(4,128)S(1)} %get-tuple-element.158), kind=kOutput, calls=%fused_computation.14.clone.1 | convolution fusion | flops 204070912 | bytes 6937600 | tf_op jit(solution)/shard_map/while/body/eval_jaxpr/hqk,khd->qhd/dot_general | solution.py:87
  141.6 0.1 copy.27
  141.7 0.7 constant_dynamic-update-slice_fusion.2
  142.4 0.6 dynamic_slice.28
  143.7 0.6 fusion.86
  144.3 0.4 constant_dynamic-slice_fusion.4
  144.7 1.7 constant_dynamic-slice_fusion.5
  146.4 6.0 %fusion.87 = (f32[4,512]{1,0:T(4,128)S(1)}, f32[4,512,766]{2,1,0:T(8,128)}) fusion(pred[512,766]{1,0:T(8,128)(4,1)S(1)} %fusion.86, bf16[512,4,64]{0,2,1:T(8,128)(2,1)} %bitcast.85, bf16[766,4,64]{0,2,1:T(8,128)(2,1)S(1)} %bitcast.83), kind=kOutput, calls=%fused_computation.94.clone.1 | convolution fusion | flops 207078144 | bytes 7329792 | tf_op jit(solution)/shard_map/while/body/eval_jaxpr/sub | solution.py:85
  152.4 3.9 %fusion.88 = bf16[4,64,512]{2,1,0:T(8,128)(2,1)S(1)} fusion(bf16[766,4,64]{0,2,1:T(8,128)(2,1)S(1)} %bitcast.82, f32[4,512,766]{2,1,0:T(8,128)} %get-tuple-element.157, f32[4,512]{1,0:T(4,128)S(1)} %get-tuple-element.158), kind=kOutput, calls=%fused_computation.14.clone.1 | convolution fusion | flops 204070912 | bytes 6937600 | tf_op jit(solution)/shard_map/while/body/eval_jaxpr/hqk,khd->qhd/dot_general | solution.py:87
  156.4 0.1 copy.27
  156.5 0.7 constant_dynamic-update-slice_fusion.2
  157.2 18.8 %all_to_all.32 = bf16[8,256,256]{2,1,0:T(8,128)(2,1)S(1)} all-to-all(bf16[8,256,256]{2,1,0:T(8,128)(2,1)} %bitcast.89), channel_id=1, replica_groups=mesh['seq'=4,'tp'=8] {'tp'}, dimensions={0} | all-to-all | bytes 2097152 | tf_op jit(solution)/shard_map/all_to_all | solution.py:95
  176.1 0.5 copy.18
  176.6 5.7 %convolution_convert_fusion = bf16[256,2048]{1,0:T(8,128)(2,1)S(1)} fusion(bf16[256,2048]{0,1:T(8,128)(2,1)S(1)} %bitcast.84, bf16[2048,2048]{1,0:T(8,128)(2,1)} %all-gather.5.cloned.1.call-done), kind=kOutput, calls=%fused_computation.43 | convolution fusion | flops 2148007936 | bytes 10485760 | tf_op jit(solution)/shard_map/dot_general | solution.py:96
  182.4 1.0 copy.25
  183.4 3.6 %all-to-all-start.1 = ((bf16[256,8,256]{2,0,1:T(8,128)(2,1)}), bf16[256,8,256]{2,0,1:T(8,128)(2,1)S(1)}, u32[]{:S(2)}, u32[]{:S(2)}) async-start(bf16[256,8,256]{2,0,1:T(8,128)(2,1)} %bitcast.65), calls=%async_computation.1 | async-start | bytes 2097152 | tf_op jit(solution)/shard_map/all_to_all | solution.py:101
  187.1 15.2 %all-to-all-done.1 = bf16[256,8,256]{2,0,1:T(8,128)(2,1)S(1)} async-done(((bf16[256,8,256]{2,0,1:T(8,128)(2,1)}), bf16[256,8,256]{2,0,1:T(8,128)(2,1)S(1)}, u32[]{:S(2)}, u32[]{:S(2)}) %all-to-all-start.1) | async-done | bytes 1048608 | tf_op jit(solution)/shard_map/all_to_all | solution.py:101
  202.3 1.6 fusion.62
  203.9 1.1 gather_fusion
  205.1 12.8 %all_gather.11 = bf16[224,2048]{1,0:T(8,128)(2,1)S(1)} all-gather(bf16[224,256]{1,0:T(8,128)(2,1)S(1)} %broadcast_select_fusion), channel_id=1, replica_groups=mesh['seq'=4,'tp'=8] {'tp'}, dimensions={1}, use_global_device_ids=true | all-gather | bytes 1032192 | tf_op jit(solution)/shard_map/all_gather | solution.py:35
  217.9 0.3 fusion.39
  218.2 9.6 %convolution_bitcast_fusion = f32[2,224,2560]{2,1,0:T(8,128)S(1)} fusion(bf16[2,2048,2560]{2,1,0:T(8,128)(2,1)} %param.16, bf16[224,2048]{1,0:T(8,128)(2,1)S(1)} %all_gather.11, f32[2048]{0:T(1024)S(1)} %convert_element_type.85, f32[224]{0:T(256)S(1)} %add_rsqrt_fusion.1), kind=kOutput, calls=%fused_computation.34 | convolution fusion | flops 4699455488 | bytes 26485632 | tf_op jit(solution)/shard_map/nd,kdf->knf/dot_general | solution.py:37
  227.7 7.8 %convolution_convert_fusion.1 = bf16[224,2048]{1,0:T(8,128)(2,1)} fusion(bf16[2560,2048]{1,0:T(8,128)(2,1)} %param.17, f32[2,224,2560]{2,1,0:T(8,128)S(1)} %convolution_bitcast_fusion), kind=kOutput, calls=%fused_computation.44 | convolution fusion | flops 2355003392 | bytes 15990784 | tf_op jit(solution)/shard_map/dot_general | solution.py:39
  235.6 0.6 dynamic_slice.23
  236.2 0.9 iota_compare_fusion
  237.1 33.6 %reduce-scatter.2.cloned.1.call-done = bf16[224,256]{1,0:T(8,128)(2,1)} async-done(((bf16[224,2048]{1,0:T(8,128)(2,1)}), bf16[224,256]{1,0:T(8,128)(2,1)}) %reduce-scatter.2.cloned.1.call-update) | async-done | bytes 114704 | tf_op jit(solution)/shard_map/reduce_scatter | solution.py:40
  270.7 5.0 %scatter_custom_fusion = f32[2048,256]{1,0:T(8,128)} fusion(f32[2048,256]{1,0:T(8,128)} %get-tuple-element.97, s32[224]{0:T(256)S(1)} %bitcast.91, bf16[224,256]{1,0:T(8,128)(2,1)} %reduce-scatter.2.cloned.1.call-done, f32[]{:T(128)} %constant.102.clone.1, pred[224]{0:T(512)(128)(4,1)S(1)} %iota_compare_fusion), kind=kCustom, calls=%fused_computation.74 | custom fusion | flops 172032 | bytes 2212864 | tf_op jit(solution)/shard_map/scatter-add | solution.py:113
  275.7 2.7 convert_element_type.90
  (40 shorter events, 0.5 us)
Async XLA Ops:
  6.5 66.6 %copy-start = (bf16[3,2048,256]{2,1,0:T(8,128)(2,1)S(1)}, bf16[3,2048,256]{2,1,0:T(8,128)(2,1)}, u32[]{:S(2)}) copy-start(bf16[3,2048,256]{2,1,0:T(8,128)(2,1)} %param.13) | copy-start | bytes 9437188
  6.5 61.4 %all-gather.3.cloned.1.call-start = ((), (), s32[]{:S(2)}) async-start(), calls=%async_computation.3 | async-start | bytes 9437184 | tf_op jit(solution)/shard_map/all_gather | solution.py:50
  7.3 169.4 %all-gather.5.cloned.1.call-start = ((), (), s32[]{:S(2)}) async-start(), calls=%async_computation.4 | async-start | bytes 9437184 | tf_op jit(solution)/shard_map/all_gather | solution.py:98
  67.9 5.8 %copy-start.2 = (bf16[2048,2048]{1,0:T(8,128)(2,1)S(1)}, bf16[2048,2048]{1,0:T(8,128)(2,1)}, u32[]{:S(2)}) copy-start(bf16[2048,2048]{1,0:T(8,128)(2,1)} %all-gather.3.cloned.1.call-done) | copy-start | bytes 25165828
  82.7 6.6 %collective-permute-start = (bf16[127,512]{0,1:T(8,128)(2,1)S(1)}, bf16[127,512]{0,1:T(8,128)(2,1)S(1)}, u32[]{:S(2)}, u32[]{:S(2)}) collective-permute-start(bf16[127,512]{0,1:T(8,128)(2,1)S(1)} %get-tuple-element.109), channel_id=1, source_target_pairs={{0,8},{8,16},{16,24},{1,9},{9,17},{17,25},{2,10},{10,18},{18,26},{... | collective-permute-start | bytes 390152 | tf_op jit(solution)/shard_map/ppermute | solution.py:18
  86.1 7.3 %collective-permute-start.1 = (bf16[127,512]{0,1:T(8,128)(2,1)S(1)}, bf16[127,512]{0,1:T(8,128)(2,1)S(1)}, u32[]{:S(2)}, u32[]{:S(2)}) collective-permute-start(bf16[127,512]{0,1:T(8,128)(2,1)S(1)} %get-tuple-element.108), channel_id=1, source_target_pairs={{8,0},{16,8},{24,16},{9,1},{17,9},{25,17},{10,2},{18,10},{26,18},{... | collective-permute-start | bytes 390152 | tf_op jit(solution)/shard_map/ppermute | solution.py:21
  182.3 4.7 %copy-start.4 = (bf16[2048]{0:T(1024)(128)(2,1)S(1)}, bf16[2048]{0:T(1024)(128)(2,1)}, u32[]{:S(2)}) copy-start(bf16[2048]{0:T(1024)(128)(2,1)} %param.15) | copy-start | bytes 12292
  182.4 4.7 %copy-start.5 = (s32[1,224]{1,0:T(1,128)S(1)}, s32[1,224]{1,0:T(1,128)}, u32[]{:S(2)}) copy-start(s32[1,224]{1,0:T(1,128)} %param.18) | copy-start | bytes 2692
  182.4 20.0 %copy-start.3 = (bf16[2048,256]{1,0:T(8,128)(2,1)S(1)}, bf16[2048,256]{1,0:T(8,128)(2,1)}, u32[]{:S(2)}) copy-start(bf16[2048,256]{1,0:T(8,128)(2,1)} %param.11) | copy-start | bytes 3145732
  183.4 18.9 %all-to-all-start.1 = ((bf16[256,8,256]{2,0,1:T(8,128)(2,1)}), bf16[256,8,256]{2,0,1:T(8,128)(2,1)S(1)}, u32[]{:S(2)}, u32[]{:S(2)}) async-start(bf16[256,8,256]{2,0,1:T(8,128)(2,1)} %bitcast.65), calls=%async_computation.1 | async-start | bytes 2097152 | tf_op jit(solution)/shard_map/all_to_all | solution.py:101
  187.0 83.7 %reduce-scatter.2.cloned.1.call-start = ((), (), s32[]{:S(2)}) async-start(), calls=%async_computation.5 | async-start | bytes 1032192 | tf_op jit(solution)/shard_map/reduce_scatter | solution.py:40
  227.7 7.9 %copy-start.6 = (s32[4]{0:T(128)S(1)}, s32[4]{0:T(128)}, u32[]{:S(2)}) copy-start(s32[4]{0:T(128)} %param.19) | copy-start | bytes 52
  235.6 42.8 %copy-start.1 = (bf16[3,2048,256]{2,1,0:T(8,128)(2,1)S(1)}, bf16[3,2048,256]{2,1,0:T(8,128)(2,1)}, u32[]{:S(2)}) copy-start(bf16[3,2048,256]{2,1,0:T(8,128)(2,1)} %param.13) | copy-start | bytes 9437188
Sparse Core Ops, SparseCore 0:
  9.2 58.6 all-gather.2
  69.8 54.4 all-gather.4
  235.7 34.9 reduce-scatter.1
where the time goes:
time: 286 us; the launch traced here: 285 us
  waiting for transfers between devices  114 us (40%)
  matrix products  70.8 us (25%)
  blocking collectives  31.6 us (11%)
  local copies, waits for them, and re-layouts  23.6 us (8%)
  other arithmetic  20.6 us (7%)
  between operations  13.3 us (5%)
  starting transfers between devices  8.33 us (3%)
    all_gather x1, waiting for transfers between devices, local(): whole = lax.all_gather(residual, 'tp', axis=1, tiled=True)  59.2 us
    reduce_scatter x1, waiting for transfers between devices, heavy_branch(): lax.psum_scatter(partial_value.astype(jnp.bfloat16), 'tp', scatter_dimens...  33.6 us
    sub x4, matrix products, attend(): expo = jnp.exp(scores - top)  24.1 us
    all_to_all x1, blocking collectives, local(): lax.all_to_all(context, 'tp', split_axis=0, concat_axis=1, tiled=True)  18.8 us
    dot_general x4, matrix products, attend(): jnp.einsum('hqk,khd->qhd', prob_rows, value_blk, preferred_element_type=j...  15.9 us
    all_to_all x1, waiting for transfers between devices, local(): lax.all_to_all(mixed_rows.astype(jnp.bfloat16), 'tp', split_axis=1, conca...  15.2 us
    all_gather x1, blocking collectives, heavy_branch(): full_rows = lax.all_gather(rows_part, 'tp', axis=1, tiled=True)  12.8 us
    dot_general x1, matrix products, heavy_branch(): jnp.einsum('nd,kdf->knf', normed_rows, ffn_in, preferred_element_type=jnp...  9.56 us
  transfers between devices with their start and end apart: 6, of which 5 were waited for; matrix products, arithmetic and copies ran while one was open for 28% of the time, Pallas kernels for 0%

commit v1 on v0

v1 whole, which is shorter than its diff:
```python
import functools

import jax
import jax.numpy as jnp
from jax import lax
from jax.experimental import pallas as pl
from jax.experimental.pallas import tpu as pltpu
from jax.sharding import PartitionSpec as P

HD = 64
RADIUS = 127
BLK = 128
VMEM_LIMIT = 56 * 1024 * 1024

epsilon = 1e-06
f32 = jnp.float32
bf16 = jnp.bfloat16

VMEM = pl.BlockSpec(memory_space=pltpu.VMEM)
SMEM = pl.BlockSpec(memory_space=pltpu.SMEM)


def params():
    return pltpu.CompilerParams(vmem_limit_bytes=VMEM_LIMIT)


class Pairs:
    def __init__(self):
        self.core = [(i, i ^ 1) for i in range(8)]
        self.first = [(i, i ^ (4 if i & 1 else 2)) for i in range(8)]
        self.second = [(i, i ^ (2 if i & 1 else 4)) for i in range(8)]

    def offsets(self, width):
        me = lax.axis_index("tp")
        first = jnp.where(me & 1 == 1, 4, 2)
        second = 6 - first
        blocks = [0, first, second, 6, 1, 1 ^ second, 1 ^ first, 7]
        return jnp.stack([(me ^ block) * width for block in blocks]).astype(jnp.int32)


def move(value, pairs):
    return lax.ppermute(value, "tp", pairs)


def gather_blocks(pairs, own):
    first = move(own, pairs.first)
    second = move(own, pairs.second)
    across = move(first, pairs.second)
    same_chip = [own, first, second, across]
    return same_chip + [move(block, pairs.core) for block in same_chip]


def add(left, right):
    return left.astype(f32) + right.astype(f32)


def reduce_blocks(pairs, keep, send):
    other = move(send, pairs.core)
    across = move(add(keep[3], other[3]).astype(bf16), pairs.first)
    near = move(add(keep[1], other[1]).astype(bf16), pairs.first)
    turned = (add(keep[2], other[2]) + across.astype(f32)).astype(bf16)
    far = move(turned, pairs.second)
    return add(keep[0], other[0]) + near.astype(f32) + far.astype(f32)


def put_normed(blocks, offsets, gain_ref, normed):
    total = None
    for block in blocks:
        wide = block[...].astype(f32)
        total = wide * wide if total is None else total + wide * wide
    width = blocks[0].shape[1]
    features = width * len(blocks)
    scale = lax.rsqrt(jnp.sum(total, axis=-1, keepdims=True) / features + epsilon)
    for number, block in enumerate(blocks):
        if len(blocks) == 1:
            columns = slice(None)
        else:
            columns = pl.ds(pl.multiple_of(offsets[number], width), width)
        gained = block[...].astype(f32) * scale * gain_ref[:, columns].astype(f32)
        normed[:, columns] = gained.astype(bf16)


def qkv_kernel(count, offsets, gain_ref, weight_ref, *refs):
    blocks, outs, normed = refs[:count], refs[count : count + 3], refs[count + 3]
    put_normed(blocks, offsets, gain_ref, normed)
    for number, out in enumerate(outs):
        value = jnp.dot(normed[...], weight_ref[number], preferred_element_type=f32)
        if number == 0:
            value = value * (1.0 / HD**0.5)
        out[...] = value.astype(bf16)


def qkv(blocks, offsets, gain_row, attn_in):
    rows, width = blocks[0].shape
    features, local_width = attn_in.shape[1:]
    count = len(blocks)
    tile = rows // 2 if rows >= 512 else rows
    out = jax.ShapeDtypeStruct((rows, local_width), bf16)
    return pl.pallas_call(
        functools.partial(qkv_kernel, count),
        grid=(rows // tile,),
        out_shape=[out] * 3,
        in_specs=[
            SMEM,
            pl.BlockSpec((1, features), lambda i: (0, 0)),
            pl.BlockSpec((3, features, local_width), lambda i: (0, 0, 0)),
        ]
        + [pl.BlockSpec((tile, width), lambda i: (i, 0))] * count,
        out_specs=[pl.BlockSpec((tile, local_width), lambda i: (i, 0))] * 3,
        scratch_shapes=[pltpu.VMEM((tile, features), bf16)],
        compiler_params=params(),
        cost_estimate=pl.CostEstimate(
            flops=2 * rows * features * 3 * local_width,
            bytes_accessed=2 * (rows * features + 3 * features * local_width + 3 * rows * local_width),
            transcendentals=0,
        ),
        name="norm_qkv",
    )(offsets, gain_row, attn_in, *blocks)


def project(rows_ref, weight_ref, offsets, outs):
    if len(outs) == 1:
        outs[0][...] = jnp.dot(rows_ref[...], weight_ref[...], preferred_element_type=f32).astype(bf16)
        return
    width = outs[0].shape[2]
    for side, out in enumerate(outs):
        for number in range(4):
            columns = pl.ds(pl.multiple_of(offsets[4 * side + number], width), width)
            value = jnp.dot(rows_ref[...], weight_ref[:, columns], preferred_element_type=f32)
            out[number] = value.astype(bf16)


def partial_shapes(split, rows, features, width):
    if split:
        return [jax.ShapeDtypeStruct((4, rows, width), bf16)] * 2
    return [jax.ShapeDtypeStruct((rows, features), bf16)]


def attention_kernel(queries, keys, n_arrays, n_outs, ends, offsets, weight_ref, *refs):
    arrays, outs, context = refs[:n_arrays], refs[n_arrays : n_arrays + n_outs], refs[-1]
    width = weight_ref.shape[0]
    heads = width // HD
    span = 3 * BLK
    row = lax.broadcasted_iota(jnp.int32, (BLK, span), 0)
    column = lax.broadcasted_iota(jnp.int32, (BLK, span), 1)
    band = (column - row >= BLK - RADIUS) & (column - row <= BLK + RADIUS)
    head_of = lax.broadcasted_iota(jnp.int32, (BLK, width), 1) // HD

    def load(kind, block):
        number, start = keys[block]
        return arrays[3 * number + kind][start : start + BLK, :]

    for place, block in enumerate(queries):
        query = load(0, block)
        stacked = jnp.concatenate(
            [jnp.where(head_of == head, query, jnp.zeros_like(query)) for head in range(heads)], axis=0
        )
        key = jnp.concatenate([load(1, block + step) for step in (-1, 0, 1)], axis=0)
        value = jnp.concatenate([load(2, block + step) for step in (-1, 0, 1)], axis=0)
        scores = lax.dot_general(stacked, key, (((1,), (1,)), ((), ())), preferred_element_type=f32)
        usable = band
        if keys[block - 1] is keys["low"]:
            usable = usable & ((column >= BLK) | (ends[0] > 0))
        if keys[block + 1] is keys["high"]:
            usable = usable & ((column < 2 * BLK) | (ends[1] > 0))
        scores = jnp.where(usable[None], scores.reshape(heads, BLK, span), -jnp.inf)
        top = jnp.max(scores, axis=-1, keepdims=True)
        expo = jnp.exp(scores - top)
        share = 1.0 / jnp.sum(expo, axis=-1, keepdims=True)
        expo = expo.astype(bf16).reshape(heads * BLK, span)
        mixed = jnp.dot(expo, value, preferred_element_type=f32).reshape(heads, BLK, width) * share
        chosen = mixed[0]
        for head in range(1, heads):
            chosen = jnp.where(head_of == head, mixed[head], chosen)
        context[place * BLK : (place + 1) * BLK, :] = chosen.astype(bf16)
    project(context, weight_ref, offsets, outs)


def attention(queries, keys, arrays, ends, offsets, attn_out, split):
    rows = len(queries) * BLK
    width, features = attn_out.shape
    flat = [piece for triple in arrays for piece in triple]
    outs = partial_shapes(split, rows, features, width)
    heads = width // HD
    return pl.pallas_call(
        functools.partial(attention_kernel, queries, keys, len(flat), len(outs)),
        out_shape=outs,
        in_specs=[SMEM, SMEM, VMEM] + [VMEM] * len(flat),
        out_specs=[VMEM] * len(outs),
        scratch_shapes=[pltpu.VMEM((rows, width), bf16)],
        compiler_params=params(),
        cost_estimate=pl.CostEstimate(
            flops=2 * rows * (2 * 3 * BLK * width * heads + width * features),
            bytes_accessed=2 * (rows * features + width * features + 6 * rows * width),
            transcendentals=rows * heads * 3 * BLK,
        ),
        name="band_attention",
    )(ends, offsets, attn_out, *flat)


def ffn_kernel(count, n_outs, steps, offsets, gain_ref, in_ref, out_weight_ref, *refs):
    blocks, outs = refs[:count], refs[count : count + n_outs]
    normed, total = refs[count + n_outs :]
    step = pl.program_id(0)

    @pl.when(step == 0)
    def start():
        put_normed(blocks, offsets, gain_ref, normed)
        total[...] = jnp.zeros_like(total)

    gate = jnp.dot(normed[...], in_ref[0], preferred_element_type=f32)
    up = jnp.dot(normed[...], in_ref[1], preferred_element_type=f32)
    hidden = (jax.nn.gelu(gate, approximate=True) * up).astype(bf16)
    total[...] += jnp.dot(hidden, out_weight_ref[...], preferred_element_type=f32)

    @pl.when(step == steps - 1)
    def finish():
        if n_outs == 1:
            outs[0][...] = total[...].astype(bf16)
        else:
            width = outs[0].shape[2]
            for side, out in enumerate(outs):
                for number in range(4):
                    columns = pl.ds(pl.multiple_of(offsets[4 * side + number], width), width)
                    out[number] = total[:, columns].astype(bf16)


def ffn(blocks, offsets, gain_row, ffn_in, ffn_out, split):
    rows, width = blocks[0].shape
    hidden, features = ffn_out.shape
    count = len(blocks)
    tile = 256 if hidden % 256 == 0 else 128
    steps = hidden // tile
    outs = partial_shapes(split, rows, features, width)
    return pl.pallas_call(
        functools.partial(ffn_kernel, count, len(outs), steps),
        grid=(steps,),
        out_shape=outs,
        in_specs=[
            SMEM,
            pl.BlockSpec((1, features), lambda i: (0, 0)),
            pl.BlockSpec((2, features, tile), lambda i: (0, 0, i)),
            pl.BlockSpec((tile, features), lambda i: (i, 0)),
        ]
        + [pl.BlockSpec((rows, width), lambda i: (0, 0))] * count,
        out_specs=[pl.BlockSpec(out.shape, lambda i, dims=len(out.shape): (0,) * dims) for out in outs],
        scratch_shapes=[pltpu.VMEM((rows, features), bf16), pltpu.VMEM((rows, features), f32)],
        compiler_params=params(),
        cost_estimate=pl.CostEstimate(
            flops=2 * rows * features * 3 * hidden,
            bytes_accessed=2 * 3 * hidden * features,
            transcendentals=rows * hidden,
        ),
        name="heavy_ffn",
    )(offsets, gain_row, ffn_in, ffn_out, *blocks)


def spread_kernel(tile, updated_ref, heavy_ref, rows_ref, used_ref, out_ref):
    slots = heavy_ref.shape[0]
    heavy = jnp.where(used_ref[...] > 0, heavy_ref[...], 0.0)
    coarse = heavy.astype(bf16)
    fine = (heavy - coarse.astype(f32)).astype(bf16)
    position = lax.broadcasted_iota(jnp.int32, (tile, slots), 0) + pl.program_id(0) * tile
    one_hot = (position == rows_ref[...]).astype(f32).astype(bf16)
    extra = jnp.dot(one_hot, coarse, preferred_element_type=f32)
    extra += jnp.dot(one_hot, fine, preferred_element_type=f32)
    out_ref[...] = (updated_ref[...].astype(f32) + extra).astype(bf16)


def spread(updated, heavy, route_rows, usable_slots):
    rows, width = updated.shape
    slots = heavy.shape[0]
    tile = min(512, rows)
    return pl.pallas_call(
        functools.partial(spread_kernel, tile),
        grid=(rows // tile,),
        out_shape=jax.ShapeDtypeStruct((rows, width), bf16),
        in_specs=[
            pl.BlockSpec((tile, width), lambda i: (i, 0)),
            pl.BlockSpec((slots, width), lambda i: (0, 0)),
            pl.BlockSpec((1, slots), lambda i: (0, 0)),
            pl.BlockSpec((slots, 1), lambda i: (0, 0)),
        ],
        out_specs=pl.BlockSpec((tile, width), lambda i: (i, 0)),
        compiler_params=params(),
        name="spread_rows",
    )(updated, heavy, route_rows, usable_slots.astype(jnp.int32)[:, None])


def plan(total):
    middle = max(2, (total - 4) // 6)
    left = (total - 4 - middle) // 2
    cut, end = 2 + left, total - 2
    chunks = [
        [0, 1, end, end + 1],
        list(range(2, cut)),
        list(range(cut + middle, end)),
        list(range(cut, cut + middle)),
    ]
    groups = [
        None,
        list(range(0, cut - 1)),
        list(range(cut + middle + 1, total)),
        list(range(cut - 1, cut + middle + 1)),
    ]
    return chunks, groups


def local(
    residual, attn_gain, attn_in, attn_out, ffn_gain, ffn_in, ffn_out, route_rows, route_counts
):
    seq_count = lax.axis_size("seq")
    seq_index = lax.axis_index("seq")
    tok_rows, width = residual.shape
    split = lax.axis_size("tp") == 8
    if split:
        pairs = Pairs()
        offsets = pairs.offsets(width)
        gather = functools.partial(gather_blocks, pairs)
        reduce = functools.partial(reduce_blocks, pairs)
    else:
        offsets = jnp.zeros((1,), jnp.int32)
        gather = lambda own: [lax.all_gather(own, "tp", axis=1, tiled=True)]
        reduce = lambda part: lax.psum_scatter(part, "tp", scatter_dimension=1, tiled=True).astype(f32)

    chunks, groups = plan(tok_rows // BLK)
    ends = jnp.stack([seq_index > 0, seq_index < seq_count - 1]).astype(jnp.int32)

    def rows_of(array, blocks):
        pieces, start = [], 0
        for at in range(1, len(blocks) + 1):
            if at == len(blocks) or blocks[at] != blocks[at - 1] + 1:
                pieces.append(array[blocks[start] * BLK : (blocks[at - 1] + 1) * BLK])
                start = at
        return pieces[0] if len(pieces) == 1 else jnp.concatenate(pieces, axis=0)

    keys, arrays, pending, updated = {}, [], [], [None] * len(chunks)
    held = []
    for number, (blocks, queries) in enumerate(zip(chunks, groups)):
        own = rows_of(residual, blocks)
        if number >= 2:
            own, _ = lax.optimization_barrier((own, held[number - 2]))
        whole = gather(own)
        held.append(whole[1] if split else whole[0])
        triple = qkv(whole, offsets, attn_gain[None], attn_in)
        for at, block in enumerate(blocks):
            keys[block] = (len(arrays), at * BLK)
        arrays.append(triple)
        if number == 0:
            up = [(i, i + 1) for i in range(seq_count - 1)]
            down = [(target, source) for source, target in up]
            low = [lax.ppermute(kind[-BLK:], "seq", up) for kind in triple[1:]]
            high = [lax.ppermute(kind[:BLK], "seq", down) for kind in triple[1:]]
            keys["low"] = keys[-1] = (len(arrays), 0)
            keys["high"] = keys[blocks[-1] + 1] = (len(arrays) + 1, 0)
            arrays.append([low[0]] + low)
            arrays.append([high[0]] + high)
        if queries is None:
            continue
        needed = sorted({keys[b + step][0] for b in queries for step in (-1, 0, 1)})
        place = {array: at for at, array in enumerate(needed)}
        inner = {name: (place.get(array), start) for name, (array, start) in keys.items()}
        inner["low"] = inner[-1]
        inner["high"] = inner[chunks[0][-1] + 1]
        parts = attention(
            queries, inner, [arrays[array] for array in needed], ends, offsets, attn_out, split
        )
        mixed = reduce(*parts)
        pending.append((queries[0], (add(rows_of(residual, queries), mixed)).astype(bf16)))
    updated = jnp.concatenate([rows for _, rows in sorted(pending, key=lambda pair: pair[0])], axis=0)

    slots = jnp.arange(route_rows.shape[1], dtype=jnp.int32)
    row_count = lax.dynamic_index_in_dim(route_counts, seq_index, 0, keepdims=False)
    taken = jnp.take(updated, route_rows[0], axis=0)
    heavy = reduce(*ffn(gather(taken), offsets, ffn_gain[None], ffn_in, ffn_out, split))
    return spread(updated, heavy, route_rows, slots < row_count)


def solution(mesh):
    in_specs = (
        P("seq", "tp"),
        P(),
        P(None, None, "tp"),
        P("tp", None),
        P(),
        P(None, None, "tp"),
        P("tp", None),
        P("seq", None),
        P(),
    )
    out_specs = P("seq", "tp")
    return jax.shard_map(local, mesh=mesh, in_specs=in_specs, out_specs=out_specs, check_vma=False)
```

time: 286 us -> 188 us (0.66)
  matrix products: 70.8 us -> 0 us
  Pallas kernels: 0 us -> 65.6 us
  waiting for transfers between devices: 114 us -> 56.4 us
  starting transfers between devices: 8.33 us -> 45.5 us
  blocking collectives: 31.6 us -> 0 us
  local copies, waits for them, and re-layouts: 23.6 us -> 10.8 us
  between operations: 13.3 us -> 0.68 us
  other arithmetic: 20.6 us -> 8.33 us
    pallas_call x0 -> x9, Pallas kernels: none -> 65.6 us  [the longest x4 25.2 us: qkv(): pl.pallas_call(functools.partial(qkv_kernel, count), grid=(rows // tile,)...]
    all_gather x2 -> x0, waiting for transfers between devices: 59.2 us -> none  [the longest x1 59.2 us: local(): whole = lax.all_gather(residual, 'tp', axis=1, tiled=True)]
    ppermute x2 -> x55, waiting for transfers between devices: 4.36 us -> 56.4 us  [the longest x51 56 us: move(): return lax.ppermute(value, 'tp', pairs)]
    dot_general x8 -> x0, matrix products: 46.7 us -> none  [the longest x4 15.9 us: attend(): jnp.einsum('hqk,khd->qhd', prob_rows, value_blk, preferred_element_type=j...]
    ppermute x2 -> x55, starting transfers between devices: 4.69 us -> 45.5 us  [the longest x51 34.9 us: move(): return lax.ppermute(value, 'tp', pairs)]
    reduce_scatter x1 -> x0, waiting for transfers between devices: 33.6 us -> none  [heavy_branch(): lax.psum_scatter(partial_value.astype(jnp.bfloat16), 'tp', scatter_dimens...]
    sub x4 -> x0, matrix products: 24.1 us -> none  [attend(): expo = jnp.exp(scores - top)]
    all_to_all x1 -> x0, blocking collectives: 18.8 us -> none  [local(): lax.all_to_all(context, 'tp', split_axis=0, concat_axis=1, tiled=True)]
  transfers between devices with their start and end apart: 6 -> 55, of which waited for: 5 -> 20; matrix products, arithmetic and copies ran while one was open for 28% -> 5% of each run, Pallas kernels for 0% -> 23%
where the time goes in v1:
time: 188 us; the launch traced here: 187 us
  Pallas kernels  65.6 us (35%)
  waiting for transfers between devices  56.4 us (30%)
  starting transfers between devices  45.5 us (24%)
  local copies, waits for them, and re-layouts  10.8 us (6%)
  other arithmetic  8.33 us (4%)
    ppermute x51, waiting for transfers between devices, move(): return lax.ppermute(value, 'tp', pairs)  56 us
    ppermute x51, starting transfers between devices, move(): return lax.ppermute(value, 'tp', pairs)  34.9 us
    pallas_call x4, Pallas kernels, qkv(): pl.pallas_call(functools.partial(qkv_kernel, count), grid=(rows // tile,)...  25.2 us
    pallas_call x1, Pallas kernels, ffn(): pl.pallas_call(functools.partial(ffn_kernel, count, len(outs), steps), gr...  18.2 us
    pallas_call x3, Pallas kernels, attention(): pl.pallas_call(functools.partial(attention_kernel, queries, keys, len(fla...  18 us
    ppermute x2, starting transfers between devices, local(): low = [lax.ppermute(kind[-BLK:], 'seq', up) for kind in triple[1:]]  7.87 us
    pallas_call x1, Pallas kernels, spread(): pl.pallas_call(functools.partial(spread_kernel, tile), grid=(rows // tile...  4.25 us
    unnamed x98, local copies, waits for them, and re-layouts  4.04 us
  transfers between devices with their start and end apart: 55, of which 20 were waited for; matrix products, arithmetic and copies ran while one was open for 5% of the time, Pallas kernels for 23%

profile of v1, /device:TPU:0, one launch (start us, length us, event | category | flops | bytes accessed | tf_op | source)
XLA Modules:
  0.0 187.4 jit_solution(13302023684648954585)
XLA Ops:
  0.0 1.2 fusion.24
  1.2 3.0 %collective-permute-start.9 = (bf16[640,256]{1,0:T(8,128)(2,1)S(1)}, bf16[640,256]{1,0:T(8,128)(2,1)S(1)}, u32[]{:S(2)}, u32[]{:S(2)}) collective-permute-start(bf16[640,256]{1,0:T(8,128)(2,1)S(1)} %get-tuple-element.60.refs_0_), channel_id=1, source_target_pairs={{0,2},{1,5},{2,0},{3,7},{4,6},{5,1},{6,4},{7,3},{8,10},{9,13},{10,... | collective-permute-start | bytes 983048 | tf_op jit(solution)/shard_map/ppermute | solution.py:42
  4.3 1.6 collective-permute-start.1
  6.4 5.6 %collective-permute-done.9.refs_1_ = bf16[640,256]{1,0:T(8,128)(2,1)S(1)} collective-permute-done((bf16[640,256]{1,0:T(8,128)(2,1)S(1)}, bf16[640,256]{1,0:T(8,128)(2,1)S(1)}, u32[]{:S(2)}, u32[]{:S(2)}) %collective-permute-start.9) | collective-permute-done | bytes 327712 | tf_op jit(solution)/shard_map/ppermute | solution.py:42
  12.1 1.6 collective-permute-done.1.refs_2_
  13.6 1.0 collective-permute-start.27
  15.0 1.2 collective-permute-start.2
  16.2 0.7 copy-done.42
  16.9 0.8 collective-permute-start.28
  17.8 1.3 collective-permute-done.27.refs_1_
  19.0 2.4 %collective-permute-start.29 = (bf16[256,256]{1,0:T(8,128)(2,1)S(1)}, bf16[256,256]{1,0:T(8,128)(2,1)S(1)}, u32[]{:S(2)}, u32[]{:S(2)}) collective-permute-start(bf16[256,256]{1,0:T(8,128)(2,1)S(1)} %collective-permute-done.27.refs_1_), channel_id=1, source_target_pairs={{0,4},{1,3},{2,6},{3,1},{4,0},{5,7},{6,2},{7,5},{8,12},{9,11},{10,... | collective-permute-start | bytes 393224 | tf_op jit(solution)/shard_map/ppermute | solution.py:42
  21.4 1.6 collective-permute-done.28.refs_2_
  23.6 0.8 collective-permute-done.29.refs_3_
  25.5 0.7 stack.47.offsets
  26.3 2.0 %collective-permute-start.10 = (bf16[640,256]{1,0:T(8,128)(2,1)S(1)}, bf16[640,256]{1,0:T(8,128)(2,1)S(1)}, u32[]{:S(2)}, u32[]{:S(2)}) collective-permute-start(bf16[640,256]{1,0:T(8,128)(2,1)S(1)} %get-tuple-element.60.refs_0_), channel_id=1, source_target_pairs={{0,4},{1,3},{2,6},{3,1},{4,0},{5,7},{6,2},{7,5},{8,12},{9,11},{10,... | collective-permute-start | bytes 983048 | tf_op jit(solution)/shard_map/ppermute | solution.py:42
  28.3 0.8 collective-permute-start.20
  29.1 1.3 collective-permute-start.11
  31.0 4.4 %norm_qkv.7 = (bf16[256,256]{1,0:T(8,128)(2,1)}, bf16[256,256]{1,0:T(8,128)(2,1)}, bf16[256,256]{1,0:T(8,128)(2,1)}) custom-call(s32[8]{0:T(128)} %stack.47.offsets, bf16[1,2048]{1,0:T(2,128)(2,1)} %broadcast_in_dim.20.gain_ref, bf16[3,2048,256]{2,1,0:T(8,128)(2,1)} %weight_ref.11, bf16[256,256]{1,0:T(8,128)(2,1)} %copy-done.5, bf16[256,256]{1,0:T(8,128)(2,1)} %copy-done.11, ...), custom_call_target="tpu_custom_call" | custom-call | flops 805306368 | bytes 4587520 | tf_op jit(solution)/shard_map/norm_qkv/pallas_call | solution.py:99
  35.4 0.8 collective-permute-start.21
  36.2 6.3 %norm_qkv.4 = (bf16[512,256]{1,0:T(8,128)(2,1)}, bf16[512,256]{1,0:T(8,128)(2,1)}, bf16[512,256]{1,0:T(8,128)(2,1)}) custom-call(s32[8]{0:T(128)} %stack.47.offsets, bf16[1,2048]{1,0:T(2,128)(2,1)} %broadcast_in_dim.20.gain_ref, bf16[3,2048,256]{2,1,0:T(8,128)(2,1)} %weight_ref.11, bf16[512,256]{1,0:T(8,128)(2,1)} %copy-done.9, ...), custom_call_target="tpu_custom_call" | custom-call | flops 1610612736 | bytes 6029312 | tf_op jit(solution)/shard_map/norm_qkv/pallas_call | solution.py:99
  43.1 1.3 collective-permute-start.22
  44.4 1.0 fusion.26
  45.4 3.5 %collective-permute-start.7 = (bf16[128,256]{1,0:T(8,128)(2,1)S(1)}, bf16[128,256]{1,0:T(8,128)(2,1)S(1)}, u32[]{:S(2)}, u32[]{:S(2)}) collective-permute-start(bf16[128,256]{1,0:T(8,128)(2,1)S(1)} %get-tuple-element.66), channel_id=1, source_target_pairs={{0,8},{8,16},{16,24},{1,9},{9,17},{17,25},{2,10},{10,18},{18,26},{... | collective-permute-start | bytes 196616 | tf_op jit(solution)/shard_map/ppermute | solution.py:352
  48.9 0.9 fusion.25
  50.8 4.4 %collective-permute-start.8 = (bf16[128,256]{1,0:T(8,128)(2,1)S(1)}, bf16[128,256]{1,0:T(8,128)(2,1)S(1)}, u32[]{:S(2)}, u32[]{:S(2)}) collective-permute-start(bf16[128,256]{1,0:T(8,128)(2,1)S(1)} %get-tuple-element.64), channel_id=1, source_target_pairs={{0,8},{8,16},{16,24},{1,9},{9,17},{17,25},{2,10},{10,18},{18,26},{... | collective-permute-start | bytes 196616 | tf_op jit(solution)/shard_map/ppermute | solution.py:352
  56.0 7.3 %norm_qkv.5 = (bf16[640,256]{1,0:T(8,128)(2,1)}, bf16[640,256]{1,0:T(8,128)(2,1)}, bf16[640,256]{1,0:T(8,128)(2,1)}) custom-call(s32[8]{0:T(128)} %stack.47.offsets, bf16[1,2048]{1,0:T(2,128)(2,1)} %broadcast_in_dim.20.gain_ref, bf16[3,2048,256]{2,1,0:T(8,128)(2,1)} %weight_ref.11, bf16[640,256]{1,0:T(8,128)(2,1)} %copy-done.8, bf16[640,256]{1,0:T(8,128)(2,1)} %copy-done.27, ...), custom_call_target="tpu_custom_call" | custom-call | flops 2013265920 | bytes 6750208 | tf_op jit(solution)/shard_map/norm_qkv/pallas_call | solution.py:99
  63.3 1.3 collective-permute-start.38
  64.6 6.4 %band_attention.3 = (bf16[4,768,256]{2,1,0:T(8,128)(2,1)}, bf16[4,768,256]{2,1,0:T(8,128)(2,1)}) custom-call(s32[2]{0:T(128)} %add_convert_fusion.8.ends, s32[8]{0:T(128)} %stack.47.offsets, bf16[256,2048]{1,0:T(8,128)(2,1)} %weight_ref.13, bf16[512,256]{1,0:T(8,128)(2,1)} %get-tuple-element.27.refs_0_, bf16[512,256]{1,0:T(8,128)(2,1)} %get-tuple-element.28.refs_1_, ...), custom_call_target="tpu_custom_call" | custom-call | flops 2013265920 | bytes 6553600 | tf_op jit(solution)/shard_map/band_attention/pallas_call | solution.py:185
  71.0 1.5 collective-permute-start.39
  73.5 0.7 copy-done.39
  74.3 7.2 %norm_qkv.6 = (bf16[640,256]{1,0:T(8,128)(2,1)}, bf16[640,256]{1,0:T(8,128)(2,1)}, bf16[640,256]{1,0:T(8,128)(2,1)}) custom-call(s32[8]{0:T(128)} %stack.47.offsets, bf16[1,2048]{1,0:T(2,128)(2,1)} %broadcast_in_dim.20.gain_ref, bf16[3,2048,256]{2,1,0:T(8,128)(2,1)} %weight_ref.11, bf16[640,256]{1,0:T(8,128)(2,1)} %copy-done.7, bf16[640,256]{1,0:T(8,128)(2,1)} %copy-done.28, ...), custom_call_target="tpu_custom_call" | custom-call | flops 2013265920 | bytes 6750208 | tf_op jit(solution)/shard_map/norm_qkv/pallas_call | solution.py:99
  82.2 6.4 %band_attention.5 = (bf16[4,768,256]{2,1,0:T(8,128)(2,1)}, bf16[4,768,256]{2,1,0:T(8,128)(2,1)}) custom-call(s32[2]{0:T(128)} %add_convert_fusion.8.ends, s32[8]{0:T(128)} %stack.47.offsets, bf16[256,2048]{1,0:T(8,128)(2,1)} %weight_ref.13, bf16[512,256]{1,0:T(8,128)(2,1)} %get-tuple-element.27.refs_0_, bf16[512,256]{1,0:T(8,128)(2,1)} %get-tuple-element.28.refs_1_, ...), custom_call_target="tpu_custom_call" | custom-call | flops 2013265920 | bytes 6553600 | tf_op jit(solution)/shard_map/band_attention/pallas_call | solution.py:185
  88.8 5.2 %band_attention.4 = (bf16[4,512,256]{2,1,0:T(8,128)(2,1)}, bf16[4,512,256]{2,1,0:T(8,128)(2,1)}) custom-call(s32[2]{0:T(128)} %add_convert_fusion.8.ends, s32[8]{0:T(128)} %stack.47.offsets, bf16[256,2048]{1,0:T(8,128)(2,1)} %weight_ref.13, bf16[640,256]{1,0:T(8,128)(2,1)} %get-tuple-element.30.refs_6_.refs_0_, ...), custom_call_target="tpu_custom_call" | custom-call | flops 1342177280 | bytes 4718592 | tf_op jit(solution)/shard_map/band_attention/pallas_call | solution.py:185
  94.3 2.6 %collective-permute-done.34 = bf16[4,512,256]{2,1,0:T(8,128)(2,1)S(1)} collective-permute-done((bf16[4,512,256]{2,1,0:T(8,128)(2,1)}, bf16[4,512,256]{2,1,0:T(8,128)(2,1)S(1)}, u32[]{:S(2)}, u32[]{:S(2)}) %collective-permute-start.34) | collective-permute-done | bytes 1048608 | tf_op jit(solution)/shard_map/ppermute | solution.py:42
  96.9 1.2 fusion.16
  98.7 1.5 collective-permute-start.36
  101.3 1.5 collective-permute-start.42
  102.8 4.6 %collective-permute-done.36 = bf16[512,256]{1,0:T(8,128)(2,1)S(1)} collective-permute-done((bf16[512,256]{1,0:T(8,128)(2,1)S(1)}, bf16[512,256]{1,0:T(8,128)(2,1)S(1)}, u32[]{:S(2)}, u32[]{:S(2)}) %collective-permute-start.36) | collective-permute-done | bytes 262176 | tf_op jit(solution)/shard_map/ppermute | solution.py:42
  107.5 0.8 collective-permute-start.37
  108.3 1.2 collective-permute-start.17
  109.5 4.1 %collective-permute-done.18 = bf16[768,256]{1,0:T(8,128)(2,1)S(1)} collective-permute-done((bf16[768,256]{1,0:T(8,128)(2,1)S(1)}, bf16[768,256]{1,0:T(8,128)(2,1)S(1)}, u32[]{:S(2)}, u32[]{:S(2)}) %collective-permute-start.18) | collective-permute-done | bytes 393248 | tf_op jit(solution)/shard_map/ppermute | solution.py:42
  114.3 4.3 %collective-permute-done.42 = bf16[768,256]{1,0:T(8,128)(2,1)S(1)} collective-permute-done((bf16[768,256]{1,0:T(8,128)(2,1)S(1)}, bf16[768,256]{1,0:T(8,128)(2,1)S(1)}, u32[]{:S(2)}, u32[]{:S(2)}) %collective-permute-start.42) | collective-permute-done | bytes 393248 | tf_op jit(solution)/shard_map/ppermute | solution.py:42
  118.6 0.7 collective-permute-start.19
  119.5 1.3 collective-permute-start.43
  121.0 4.0 %collective-permute-done.17 = bf16[768,256]{1,0:T(8,128)(2,1)S(1)} collective-permute-done((bf16[768,256]{1,0:T(8,128)(2,1)S(1)}, bf16[768,256]{1,0:T(8,128)(2,1)S(1)}, u32[]{:S(2)}, u32[]{:S(2)}) %collective-permute-start.17) | collective-permute-done | bytes 393248 | tf_op jit(solution)/shard_map/ppermute | solution.py:42
  125.0 8.4 %collective-permute-done.41 = bf16[768,256]{1,0:T(8,128)(2,1)S(1)} collective-permute-done((bf16[768,256]{1,0:T(8,128)(2,1)S(1)}, bf16[768,256]{1,0:T(8,128)(2,1)S(1)}, u32[]{:S(2)}, u32[]{:S(2)}) %collective-permute-start.41) | collective-permute-done | bytes 393248 | tf_op jit(solution)/shard_map/ppermute | solution.py:42
  133.4 1.3 collective-permute-done.43
  135.3 1.1 gather_fusion
  137.1 1.4 collective-permute-start.45
  138.6 4.0 %collective-permute-done.44.refs_1_ = bf16[224,256]{1,0:T(8,128)(2,1)S(1)} collective-permute-done((bf16[224,256]{1,0:T(8,128)(2,1)S(1)}, bf16[224,256]{1,0:T(8,128)(2,1)S(1)}, u32[]{:S(2)}, u32[]{:S(2)}) %collective-permute-start.44) | collective-permute-done | bytes 114720 | tf_op jit(solution)/shard_map/ppermute | solution.py:42
  143.4 3.9 %collective-permute-done.46.refs_3_ = bf16[224,256]{1,0:T(8,128)(2,1)S(1)} collective-permute-done((bf16[224,256]{1,0:T(8,128)(2,1)S(1)}, bf16[224,256]{1,0:T(8,128)(2,1)S(1)}, u32[]{:S(2)}, u32[]{:S(2)}) %collective-permute-start.46) | collective-permute-done | bytes 114720 | tf_op jit(solution)/shard_map/ppermute | solution.py:42
  147.3 0.6 broadcast_in_dim.21.gain_ref
  148.0 0.6 collective-permute-done.50.refs_7_
  148.7 0.6 copy-done.23
  149.4 18.2 %heavy_ffn.1 = (bf16[4,224,256]{2,1,0:T(8,128)(2,1)}, bf16[4,224,256]{2,1,0:T(8,128)(2,1)}) custom-call(s32[8]{0:T(128)} %stack.47.offsets, bf16[1,2048]{1,0:T(2,128)(2,1)} %broadcast_in_dim.21.gain_ref, bf16[2,2048,2560]{2,1,0:T(8,128)(2,1)} %in_ref.1, bf16[2560,2048]{1,0:T(8,128)(2,1)} %out_weight_ref.1, bf16[224,256]{1,0:T(8,128)(2,1)} %copy-done.6, ...), custom_call_target="tpu_custom_call" | custom-call | flops 7046430720 | bytes 31457280 | tf_op jit(solution)/shard_map/heavy_ffn/pallas_call | solution.py:235
  168.1 1.7 collective-permute-done.51
  169.8 1.0 fusion.20
  171.5 2.0 %collective-permute-start.52 = (bf16[224,256]{1,0:T(8,128)(2,1)S(1)}, bf16[224,256]{1,0:T(8,128)(2,1)S(1)}, u32[]{:S(2)}, u32[]{:S(2)}) collective-permute-start(bf16[224,256]{1,0:T(8,128)(2,1)S(1)} %get-tuple-element.62), channel_id=1, source_target_pairs={{0,2},{1,5},{2,0},{3,7},{4,6},{5,1},{6,4},{7,3},{8,10},{9,13},{10,... | collective-permute-start | bytes 344072 | tf_op jit(solution)/shard_map/ppermute | solution.py:42
  173.5 2.2 %collective-permute-done.53 = bf16[224,256]{1,0:T(8,128)(2,1)S(1)} collective-permute-done((bf16[224,256]{1,0:T(8,128)(2,1)S(1)}, bf16[224,256]{1,0:T(8,128)(2,1)S(1)}, u32[]{:S(2)}, u32[]{:S(2)}) %collective-permute-start.53) | collective-permute-done | bytes 114720 | tf_op jit(solution)/shard_map/ppermute | solution.py:42
  175.7 0.9 fusion.18
  177.0 1.3 fusion.22.used_ref
  178.3 3.2 %collective-permute-done.54 = bf16[224,256]{1,0:T(8,128)(2,1)S(1)} collective-permute-done((bf16[224,256]{1,0:T(8,128)(2,1)S(1)}, bf16[224,256]{1,0:T(8,128)(2,1)S(1)}, u32[]{:S(2)}, u32[]{:S(2)}) %collective-permute-start.54) | collective-permute-done | bytes 114720 | tf_op jit(solution)/shard_map/ppermute | solution.py:42
  181.5 1.7 fusion.19.heavy_ref
  183.1 4.2 %spread_rows.1 = bf16[2048,256]{1,0:T(8,128)(2,1)} custom-call(bf16[2048,256]{1,0:T(8,128)(2,1)} %copy-done, f32[224,256]{1,0:T(8,128)} %fusion.19.heavy_ref, s32[1,224]{1,0:T(1,128)} %rows_ref.1, s32[224,1]{1,0:T(8,128)} %fusion.22.used_ref), custom_call_target="tpu_custom_call" | custom-call | tf_op jit(solution)/shard_map/spread_rows/pallas_call | solution.py:274
  (181 shorter events, 14.5 us)
Async XLA Ops:
  0.0 24.9 %copy-start.25 = (bf16[2048]{0:T(1024)(128)(2,1)S(1)}, bf16[2048]{0:T(1024)(128)(2,1)}, u32[]{:S(2)}) copy-start(bf16[2048]{0:T(1024)(128)(2,1)} %param.10) | copy-start | bytes 12292
  1.2 34.2 %copy-start.8 = (bf16[640,256]{1,0:T(8,128)(2,1)}, bf16[640,256]{1,0:T(8,128)(2,1)S(1)}, u32[]{:S(2)}) copy-start(bf16[640,256]{1,0:T(8,128)(2,1)S(1)} %get-tuple-element.60.refs_0_) | copy-start | bytes 983044
  1.2 48.6 %copy-start.7 = (bf16[640,256]{1,0:T(8,128)(2,1)}, bf16[640,256]{1,0:T(8,128)(2,1)S(1)}, u32[]{:S(2)}) copy-start(bf16[640,256]{1,0:T(8,128)(2,1)S(1)} %get-tuple-element.35.refs_0_) | copy-start | bytes 983044
  1.2 10.8 %collective-permute-start.9 = (bf16[640,256]{1,0:T(8,128)(2,1)S(1)}, bf16[640,256]{1,0:T(8,128)(2,1)S(1)}, u32[]{:S(2)}, u32[]{:S(2)}) collective-permute-start(bf16[640,256]{1,0:T(8,128)(2,1)S(1)} %get-tuple-element.60.refs_0_), channel_id=1, source_target_pairs={{0,2},{1,5},{2,0},{3,7},{4,6},{5,1},{6,4},{7,3},{8,10},{9,13},{10,... | collective-permute-start | bytes 983048 | tf_op jit(solution)/shard_map/ppermute | solution.py:42
  4.3 26.7 %copy-start.5 = (bf16[256,256]{1,0:T(8,128)(2,1)}, bf16[256,256]{1,0:T(8,128)(2,1)S(1)}, u32[]{:S(2)}) copy-start(bf16[256,256]{1,0:T(8,128)(2,1)S(1)} %get-tuple-element.39.refs_0_) | copy-start | bytes 393220
  4.3 31.1 %copy-start.9 = (bf16[512,256]{1,0:T(8,128)(2,1)}, bf16[512,256]{1,0:T(8,128)(2,1)S(1)}, u32[]{:S(2)}) copy-start(bf16[512,256]{1,0:T(8,128)(2,1)S(1)} %pad_maximum_fusion.1.refs_0_) | copy-start | bytes 786436
  4.3 9.3 %collective-permute-start.1 = (bf16[512,256]{1,0:T(8,128)(2,1)S(1)}, bf16[512,256]{1,0:T(8,128)(2,1)S(1)}, u32[]{:S(2)}, u32[]{:S(2)}) collective-permute-start(bf16[512,256]{1,0:T(8,128)(2,1)S(1)} %pad_maximum_fusion.1.refs_0_), channel_id=1, source_target_pairs={{0,4},{1,3},{2,6},{3,1},{4,0},{5,7},{6,2},{7,5},{8,12},{9,11},{10,... | collective-permute-start | bytes 786440 | tf_op jit(solution)/shard_map/ppermute | solution.py:42
  5.9 9.1 %collective-permute-start = (bf16[512,256]{1,0:T(8,128)(2,1)S(1)}, bf16[512,256]{1,0:T(8,128)(2,1)}, u32[]{:S(2)}, u32[]{:S(2)}) collective-permute-start(bf16[512,256]{1,0:T(8,128)(2,1)S(1)} %pad_maximum_fusion.1.refs_0_), channel_id=1, source_target_pairs={{0,2},{1,5},{2,0},{3,7},{4,6},{5,1},{6,4},{7,3},{8,10},{9,13},{10,... | collective-permute-start | bytes 786440 | tf_op jit(solution)/shard_map/ppermute | solution.py:42
  6.4 9.8 %collective-permute-start.3 = (bf16[512,256]{1,0:T(8,128)(2,1)S(1)}, bf16[512,256]{1,0:T(8,128)(2,1)S(1)}, u32[]{:S(2)}, u32[]{:S(2)}) collective-permute-start(bf16[512,256]{1,0:T(8,128)(2,1)S(1)} %pad_maximum_fusion.1.refs_0_), channel_id=1, source_target_pairs={{0,1},{1,0},{2,3},{3,2},{4,5},{5,4},{6,7},{7,6},{8,9},{9,8},{10,11... | collective-permute-start | bytes 786440 | tf_op jit(solution)/shard_map/ppermute | solution.py:42
  12.1 30.5 %copy-start.27 = (bf16[640,256]{1,0:T(8,128)(2,1)}, bf16[640,256]{1,0:T(8,128)(2,1)S(1)}, u32[]{:S(2)}) copy-start(bf16[640,256]{1,0:T(8,128)(2,1)S(1)} %collective-permute-done.9.refs_1_) | copy-start | bytes 983044
  12.1 4.9 %collective-permute-start.30 = (bf16[256,256]{1,0:T(8,128)(2,1)S(1)}, bf16[256,256]{1,0:T(8,128)(2,1)S(1)}, u32[]{:S(2)}, u32[]{:S(2)}) collective-permute-start(bf16[256,256]{1,0:T(8,128)(2,1)S(1)} %get-tuple-element.39.refs_0_), channel_id=1, source_target_pairs={{0,1},{1,0},{2,3},{3,2},{4,5},{5,4},{6,7},{7,6},{8,9},{9,8},{10,11... | collective-permute-start | bytes 393224 | tf_op jit(solution)/shard_map/ppermute | solution.py:42
  13.6 9.4 %collective-permute-start.5 = (bf16[512,256]{1,0:T(8,128)(2,1)S(1)}, bf16[512,256]{1,0:T(8,128)(2,1)S(1)}, u32[]{:S(2)}, u32[]{:S(2)}) collective-permute-start(bf16[512,256]{1,0:T(8,128)(2,1)S(1)} %collective-permute-done.1.refs_2_), channel_id=1, source_target_pairs={{0,1},{1,0},{2,3},{3,2},{4,5},{5,4},{6,7},{7,6},{8,9},{9,8},{10,11... | collective-permute-start | bytes 786440 | tf_op jit(solution)/shard_map/ppermute | solution.py:42
  13.6 5.4 %collective-permute-start.27 = (bf16[256,256]{1,0:T(8,128)(2,1)S(1)}, bf16[256,256]{1,0:T(8,128)(2,1)S(1)}, u32[]{:S(2)}, u32[]{:S(2)}) collective-permute-start(bf16[256,256]{1,0:T(8,128)(2,1)S(1)} %get-tuple-element.39.refs_0_), channel_id=1, source_target_pairs={{0,2},{1,5},{2,0},{3,7},{4,6},{5,1},{6,4},{7,3},{8,10},{9,13},{10,... | collective-permute-start | bytes 393224 | tf_op jit(solution)/shard_map/ppermute | solution.py:42
  15.0 9.4 %collective-permute-start.2 = (bf16[512,256]{1,0:T(8,128)(2,1)}, bf16[512,256]{1,0:T(8,128)(2,1)}, u32[]{:S(2)}, u32[]{:S(2)}) collective-permute-start(bf16[512,256]{1,0:T(8,128)(2,1)} %collective-permute-done.refs_1_), channel_id=1, source_target_pairs={{0,4},{1,3},{2,6},{3,1},{4,0},{5,7},{6,2},{7,5},{8,12},{9,11},{10,... | collective-permute-start | bytes 786440 | tf_op jit(solution)/shard_map/ppermute | solution.py:42
  16.2 10.0 %collective-permute-start.4 = (bf16[512,256]{1,0:T(8,128)(2,1)}, bf16[512,256]{1,0:T(8,128)(2,1)}, u32[]{:S(2)}, u32[]{:S(2)}) collective-permute-start(bf16[512,256]{1,0:T(8,128)(2,1)} %collective-permute-done.refs_1_), channel_id=1, source_target_pairs={{0,1},{1,0},{2,3},{3,2},{4,5},{5,4},{6,7},{7,6},{8,9},{9,8},{10,11... | collective-permute-start | bytes 786440 | tf_op jit(solution)/shard_map/ppermute | solution.py:42
  16.9 6.1 %collective-permute-start.28 = (bf16[256,256]{1,0:T(8,128)(2,1)S(1)}, bf16[256,256]{1,0:T(8,128)(2,1)S(1)}, u32[]{:S(2)}, u32[]{:S(2)}) collective-permute-start(bf16[256,256]{1,0:T(8,128)(2,1)S(1)} %get-tuple-element.39.refs_0_), channel_id=1, source_target_pairs={{0,4},{1,3},{2,6},{3,1},{4,0},{5,7},{6,2},{7,5},{8,12},{9,11},{10,... | collective-permute-start | bytes 393224 | tf_op jit(solution)/shard_map/ppermute | solution.py:42
  19.0 5.4 %collective-permute-start.29 = (bf16[256,256]{1,0:T(8,128)(2,1)S(1)}, bf16[256,256]{1,0:T(8,128)(2,1)S(1)}, u32[]{:S(2)}, u32[]{:S(2)}) collective-permute-start(bf16[256,256]{1,0:T(8,128)(2,1)S(1)} %collective-permute-done.27.refs_1_), channel_id=1, source_target_pairs={{0,4},{1,3},{2,6},{3,1},{4,0},{5,7},{6,2},{7,5},{8,12},{9,11},{10,... | collective-permute-start | bytes 393224 | tf_op jit(solution)/shard_map/ppermute | solution.py:42
  23.0 3.3 %collective-permute-start.32 = (bf16[256,256]{1,0:T(8,128)(2,1)S(1)}, bf16[256,256]{1,0:T(8,128)(2,1)S(1)}, u32[]{:S(2)}, u32[]{:S(2)}) collective-permute-start(bf16[256,256]{1,0:T(8,128)(2,1)S(1)} %collective-permute-done.28.refs_2_), channel_id=1, source_target_pairs={{0,1},{1,0},{2,3},{3,2},{4,5},{5,4},{6,7},{7,6},{8,9},{9,8},{10,11... | collective-permute-start | bytes 393224 | tf_op jit(solution)/shard_map/ppermute | solution.py:42
  23.0 5.2 %collective-permute-start.31 = (bf16[256,256]{1,0:T(8,128)(2,1)S(1)}, bf16[256,256]{1,0:T(8,128)(2,1)S(1)}, u32[]{:S(2)}, u32[]{:S(2)}) collective-permute-start(bf16[256,256]{1,0:T(8,128)(2,1)S(1)} %collective-permute-done.27.refs_1_), channel_id=1, source_target_pairs={{0,1},{1,0},{2,3},{3,2},{4,5},{5,4},{6,7},{7,6},{8,9},{9,8},{10,11... | collective-permute-start | bytes 393224 | tf_op jit(solution)/shard_map/ppermute | solution.py:42
  24.4 4.7 %collective-permute-start.33 = (bf16[256,256]{1,0:T(8,128)(2,1)S(1)}, bf16[256,256]{1,0:T(8,128)(2,1)S(1)}, u32[]{:S(2)}, u32[]{:S(2)}) collective-permute-start(bf16[256,256]{1,0:T(8,128)(2,1)S(1)} %collective-permute-done.29.refs_3_), channel_id=1, source_target_pairs={{0,1},{1,0},{2,3},{3,2},{4,5},{5,4},{6,7},{7,6},{8,9},{9,8},{10,11... | collective-permute-start | bytes 393224 | tf_op jit(solution)/shard_map/ppermute | solution.py:42
  24.4 11.0 %collective-permute-start.6 = (bf16[512,256]{1,0:T(8,128)(2,1)}, bf16[512,256]{1,0:T(8,128)(2,1)}, u32[]{:S(2)}, u32[]{:S(2)}) collective-permute-start(bf16[512,256]{1,0:T(8,128)(2,1)} %collective-permute-done.2.refs_3_), channel_id=1, source_target_pairs={{0,1},{1,0},{2,3},{3,2},{4,5},{5,4},{6,7},{7,6},{8,9},{9,8},{10,11... | collective-permute-start | bytes 786440 | tf_op jit(solution)/shard_map/ppermute | solution.py:42
  26.2 16.3 %collective-permute-start.12 = (bf16[640,256]{1,0:T(8,128)(2,1)S(1)}, bf16[640,256]{1,0:T(8,128)(2,1)S(1)}, u32[]{:S(2)}, u32[]{:S(2)}) collective-permute-start(bf16[640,256]{1,0:T(8,128)(2,1)S(1)} %get-tuple-element.60.refs_0_), channel_id=1, source_target_pairs={{0,1},{1,0},{2,3},{3,2},{4,5},{5,4},{6,7},{7,6},{8,9},{9,8},{10,11... | collective-permute-start | bytes 983048 | tf_op jit(solution)/shard_map/ppermute | solution.py:42
  26.3 16.3 %collective-permute-start.10 = (bf16[640,256]{1,0:T(8,128)(2,1)S(1)}, bf16[640,256]{1,0:T(8,128)(2,1)S(1)}, u32[]{:S(2)}, u32[]{:S(2)}) collective-permute-start(bf16[640,256]{1,0:T(8,128)(2,1)S(1)} %get-tuple-element.60.refs_0_), channel_id=1, source_target_pairs={{0,4},{1,3},{2,6},{3,1},{4,0},{5,7},{6,2},{7,5},{8,12},{9,11},{10,... | collective-permute-start | bytes 983048 | tf_op jit(solution)/shard_map/ppermute | solution.py:42
  28.3 14.9 %collective-permute-start.20 = (bf16[640,256]{1,0:T(8,128)(2,1)S(1)}, bf16[640,256]{1,0:T(8,128)(2,1)S(1)}, u32[]{:S(2)}, u32[]{:S(2)}) collective-permute-start(bf16[640,256]{1,0:T(8,128)(2,1)S(1)} %get-tuple-element.35.refs_0_), channel_id=1, source_target_pairs={{0,2},{1,5},{2,0},{3,7},{4,6},{5,1},{6,4},{7,3},{8,10},{9,13},{10,... | collective-permute-start | bytes 983048 | tf_op jit(solution)/shard_map/ppermute | solution.py:42
  29.1 15.3 %collective-permute-start.11 = (bf16[640,256]{1,0:T(8,128)(2,1)S(1)}, bf16[640,256]{1,0:T(8,128)(2,1)S(1)}, u32[]{:S(2)}, u32[]{:S(2)}) collective-permute-start(bf16[640,256]{1,0:T(8,128)(2,1)S(1)} %collective-permute-done.9.refs_1_), channel_id=1, source_target_pairs={{0,4},{1,3},{2,6},{3,1},{4,0},{5,7},{6,2},{7,5},{8,12},{9,11},{10,... | collective-permute-start | bytes 983048 | tf_op jit(solution)/shard_map/ppermute | solution.py:42
  35.4 10.0 %collective-permute-start.21 = (bf16[640,256]{1,0:T(8,128)(2,1)S(1)}, bf16[640,256]{1,0:T(8,128)(2,1)S(1)}, u32[]{:S(2)}, u32[]{:S(2)}) collective-permute-start(bf16[640,256]{1,0:T(8,128)(2,1)S(1)} %get-tuple-element.35.refs_0_), channel_id=1, source_target_pairs={{0,4},{1,3},{2,6},{3,1},{4,0},{5,7},{6,2},{7,5},{8,12},{9,11},{10,... | collective-permute-start | bytes 983048 | tf_op jit(solution)/shard_map/ppermute | solution.py:42
  42.5 7.5 %collective-permute-start.13 = (bf16[640,256]{1,0:T(8,128)(2,1)S(1)}, bf16[640,256]{1,0:T(8,128)(2,1)S(1)}, u32[]{:S(2)}, u32[]{:S(2)}) collective-permute-start(bf16[640,256]{1,0:T(8,128)(2,1)S(1)} %collective-permute-done.9.refs_1_), channel_id=1, source_target_pairs={{0,1},{1,0},{2,3},{3,2},{4,5},{5,4},{6,7},{7,6},{8,9},{9,8},{10,11... | collective-permute-start | bytes 983048 | tf_op jit(solution)/shard_map/ppermute | solution.py:42
  42.6 7.2 %collective-permute-start.14 = (bf16[640,256]{1,0:T(8,128)(2,1)S(1)}, bf16[640,256]{1,0:T(8,128)(2,1)S(1)}, u32[]{:S(2)}, u32[]{:S(2)}) collective-permute-start(bf16[640,256]{1,0:T(8,128)(2,1)S(1)} %collective-permute-done.10.refs_2_), channel_id=1, source_target_pairs={{0,1},{1,0},{2,3},{3,2},{4,5},{5,4},{6,7},{7,6},{8,9},{9,8},{10,11... | collective-permute-start | bytes 983048 | tf_op jit(solution)/shard_map/ppermute | solution.py:42
  43.1 20.1 %copy-start.28 = (bf16[640,256]{1,0:T(8,128)(2,1)}, bf16[640,256]{1,0:T(8,128)(2,1)S(1)}, u32[]{:S(2)}) copy-start(bf16[640,256]{1,0:T(8,128)(2,1)S(1)} %collective-permute-done.20.refs_1_) | copy-start | bytes 983044
  43.1 7.7 %collective-permute-start.22 = (bf16[640,256]{1,0:T(8,128)(2,1)S(1)}, bf16[640,256]{1,0:T(8,128)(2,1)S(1)}, u32[]{:S(2)}, u32[]{:S(2)}) collective-permute-start(bf16[640,256]{1,0:T(8,128)(2,1)S(1)} %collective-permute-done.20.refs_1_), channel_id=1, source_target_pairs={{0,4},{1,3},{2,6},{3,1},{4,0},{5,7},{6,2},{7,5},{8,12},{9,11},{10,... | collective-permute-start | bytes 983048 | tf_op jit(solution)/shard_map/ppermute | solution.py:42
  44.4 10.8 %collective-permute-start.15 = (bf16[640,256]{1,0:T(8,128)(2,1)S(1)}, bf16[640,256]{1,0:T(8,128)(2,1)S(1)}, u32[]{:S(2)}, u32[]{:S(2)}) collective-permute-start(bf16[640,256]{1,0:T(8,128)(2,1)S(1)} %collective-permute-done.11.refs_3_), channel_id=1, source_target_pairs={{0,1},{1,0},{2,3},{3,2},{4,5},{5,4},{6,7},{7,6},{8,9},{9,8},{10,11... | collective-permute-start | bytes 983048 | tf_op jit(solution)/shard_map/ppermute | solution.py:42
  45.4 5.4 %collective-permute-start.7 = (bf16[128,256]{1,0:T(8,128)(2,1)S(1)}, bf16[128,256]{1,0:T(8,128)(2,1)S(1)}, u32[]{:S(2)}, u32[]{:S(2)}) collective-permute-start(bf16[128,256]{1,0:T(8,128)(2,1)S(1)} %get-tuple-element.66), channel_id=1, source_target_pairs={{0,8},{8,16},{16,24},{1,9},{9,17},{17,25},{2,10},{10,18},{18,26},{... | collective-permute-start | bytes 196616 | tf_op jit(solution)/shard_map/ppermute | solution.py:352
  49.9 21.1 %collective-permute-start.23 = (bf16[640,256]{1,0:T(8,128)(2,1)S(1)}, bf16[640,256]{1,0:T(8,128)(2,1)S(1)}, u32[]{:S(2)}, u32[]{:S(2)}) collective-permute-start(bf16[640,256]{1,0:T(8,128)(2,1)S(1)} %get-tuple-element.35.refs_0_), channel_id=1, source_target_pairs={{0,1},{1,0},{2,3},{3,2},{4,5},{5,4},{6,7},{7,6},{8,9},{9,8},{10,11... | collective-permute-start | bytes 983048 | tf_op jit(solution)/shard_map/ppermute | solution.py:42
  50.0 22.8 %collective-permute-start.24 = (bf16[640,256]{1,0:T(8,128)(2,1)S(1)}, bf16[640,256]{1,0:T(8,128)(2,1)S(1)}, u32[]{:S(2)}, u32[]{:S(2)}) collective-permute-start(bf16[640,256]{1,0:T(8,128)(2,1)S(1)} %collective-permute-done.20.refs_1_), channel_id=1, source_target_pairs={{0,1},{1,0},{2,3},{3,2},{4,5},{5,4},{6,7},{7,6},{8,9},{9,8},{10,11... | collective-permute-start | bytes 983048 | tf_op jit(solution)/shard_map/ppermute | solution.py:42
  50.8 21.6 %collective-permute-start.25 = (bf16[640,256]{1,0:T(8,128)(2,1)S(1)}, bf16[640,256]{1,0:T(8,128)(2,1)S(1)}, u32[]{:S(2)}, u32[]{:S(2)}) collective-permute-start(bf16[640,256]{1,0:T(8,128)(2,1)S(1)} %collective-permute-done.21.refs_2_), channel_id=1, source_target_pairs={{0,1},{1,0},{2,3},{3,2},{4,5},{5,4},{6,7},{7,6},{8,9},{9,8},{10,11... | collective-permute-start | bytes 983048 | tf_op jit(solution)/shard_map/ppermute | solution.py:42
  50.8 12.4 %collective-permute-start.8 = (bf16[128,256]{1,0:T(8,128)(2,1)S(1)}, bf16[128,256]{1,0:T(8,128)(2,1)S(1)}, u32[]{:S(2)}, u32[]{:S(2)}) collective-permute-start(bf16[128,256]{1,0:T(8,128)(2,1)S(1)} %get-tuple-element.64), channel_id=1, source_target_pairs={{0,8},{8,16},{16,24},{1,9},{9,17},{17,25},{2,10},{10,18},{18,26},{... | collective-permute-start | bytes 196616 | tf_op jit(solution)/shard_map/ppermute | solution.py:352
  55.2 17.5 %collective-permute-start.26 = (bf16[640,256]{1,0:T(8,128)(2,1)S(1)}, bf16[640,256]{1,0:T(8,128)(2,1)S(1)}, u32[]{:S(2)}, u32[]{:S(2)}) collective-permute-start(bf16[640,256]{1,0:T(8,128)(2,1)S(1)} %collective-permute-done.22.refs_3_), channel_id=1, source_target_pairs={{0,1},{1,0},{2,3},{3,2},{4,5},{5,4},{6,7},{7,6},{8,9},{9,8},{10,11... | collective-permute-start | bytes 983048 | tf_op jit(solution)/shard_map/ppermute | solution.py:42
  63.3 18.2 %collective-permute-start.38 = (bf16[128,256]{1,0:T(8,128)(2,1)S(1)}, bf16[128,256]{1,0:T(8,128)(2,1)S(1)}, u32[]{:S(2)}, u32[]{:S(2)}) collective-permute-start(bf16[128,256]{1,0:T(8,128)(2,1)S(1)} %get-tuple-element.67), channel_id=1, source_target_pairs={{8,0},{16,8},{24,16},{9,1},{17,9},{25,17},{10,2},{18,10},{26,18},{... | collective-permute-start | bytes 196616 | tf_op jit(solution)/shard_map/ppermute | solution.py:353
  71.0 10.5 %collective-permute-start.39 = (bf16[128,256]{1,0:T(8,128)(2,1)S(1)}, bf16[128,256]{1,0:T(8,128)(2,1)S(1)}, u32[]{:S(2)}, u32[]{:S(2)}) collective-permute-start(bf16[128,256]{1,0:T(8,128)(2,1)S(1)} %get-tuple-element.65), channel_id=1, source_target_pairs={{8,0},{16,8},{24,16},{9,1},{17,9},{25,17},{10,2},{18,10},{26,18},{... | collective-permute-start | bytes 196616 | tf_op jit(solution)/shard_map/ppermute | solution.py:353
  72.5 27.7 %collective-permute-start.16 = (bf16[4,768,256]{2,1,0:T(8,128)(2,1)}, bf16[4,768,256]{2,1,0:T(8,128)(2,1)S(1)}, u32[]{:S(2)}, u32[]{:S(2)}) collective-permute-start(bf16[4,768,256]{2,1,0:T(8,128)(2,1)} %get-tuple-element.34), channel_id=1, source_target_pairs={{0,1},{1,0},{2,3},{3,2},{4,5},{5,4},{6,7},{7,6},{8,9},{9,8},{10,11... | collective-permute-start | bytes 4718600 | tf_op jit(solution)/shard_map/ppermute | solution.py:42
  88.5 12.5 %collective-permute-start.40 = (bf16[4,768,256]{2,1,0:T(8,128)(2,1)}, bf16[4,768,256]{2,1,0:T(8,128)(2,1)S(1)}, u32[]{:S(2)}, u32[]{:S(2)}) collective-permute-start(bf16[4,768,256]{2,1,0:T(8,128)(2,1)} %get-tuple-element.46), channel_id=1, source_target_pairs={{0,1},{1,0},{2,3},{3,2},{4,5},{5,4},{6,7},{7,6},{8,9},{9,8},{10,11... | collective-permute-start | bytes 4718600 | tf_op jit(solution)/shard_map/ppermute | solution.py:42
  94.1 2.9 %collective-permute-start.34 = (bf16[4,512,256]{2,1,0:T(8,128)(2,1)}, bf16[4,512,256]{2,1,0:T(8,128)(2,1)S(1)}, u32[]{:S(2)}, u32[]{:S(2)}) collective-permute-start(bf16[4,512,256]{2,1,0:T(8,128)(2,1)} %get-tuple-element.44), channel_id=1, source_target_pairs={{0,1},{1,0},{2,3},{3,2},{4,5},{5,4},{6,7},{7,6},{8,9},{9,8},{10,11... | collective-permute-start | bytes 3145736 | tf_op jit(solution)/shard_map/ppermute | solution.py:42
  98.1 21.4 %collective-permute-start.35 = (bf16[512,256]{1,0:T(8,128)(2,1)S(1)}, bf16[512,256]{1,0:T(8,128)(2,1)S(1)}, u32[]{:S(2)}, u32[]{:S(2)}) collective-permute-start(bf16[512,256]{1,0:T(8,128)(2,1)S(1)} %get-tuple-element.53), channel_id=1, source_target_pairs={{0,2},{1,5},{2,0},{3,7},{4,6},{5,1},{6,4},{7,3},{8,10},{9,13},{10,... | collective-permute-start | bytes 786440 | tf_op jit(solution)/shard_map/ppermute | solution.py:42
  98.7 8.6 %collective-permute-start.36 = (bf16[512,256]{1,0:T(8,128)(2,1)S(1)}, bf16[512,256]{1,0:T(8,128)(2,1)S(1)}, u32[]{:S(2)}, u32[]{:S(2)}) collective-permute-start(bf16[512,256]{1,0:T(8,128)(2,1)S(1)} %get-tuple-element.54), channel_id=1, source_target_pairs={{0,2},{1,5},{2,0},{3,7},{4,6},{5,1},{6,4},{7,3},{8,10},{9,13},{10,... | collective-permute-start | bytes 786440 | tf_op jit(solution)/shard_map/ppermute | solution.py:42
  100.4 13.2 %collective-permute-start.18 = (bf16[768,256]{1,0:T(8,128)(2,1)S(1)}, bf16[768,256]{1,0:T(8,128)(2,1)S(1)}, u32[]{:S(2)}, u32[]{:S(2)}) collective-permute-start(bf16[768,256]{1,0:T(8,128)(2,1)S(1)} %get-tuple-element.50), channel_id=1, source_target_pairs={{0,2},{1,5},{2,0},{3,7},{4,6},{5,1},{6,4},{7,3},{8,10},{9,13},{10,... | collective-permute-start | bytes 1179656 | tf_op jit(solution)/shard_map/ppermute | solution.py:42
  101.3 17.3 %collective-permute-start.42 = (bf16[768,256]{1,0:T(8,128)(2,1)S(1)}, bf16[768,256]{1,0:T(8,128)(2,1)S(1)}, u32[]{:S(2)}, u32[]{:S(2)}) collective-permute-start(bf16[768,256]{1,0:T(8,128)(2,1)S(1)} %get-tuple-element.52), channel_id=1, source_target_pairs={{0,2},{1,5},{2,0},{3,7},{4,6},{5,1},{6,4},{7,3},{8,10},{9,13},{10,... | collective-permute-start | bytes 1179656 | tf_op jit(solution)/shard_map/ppermute | solution.py:42
  107.5 13.4 %collective-permute-start.37 = (bf16[512,256]{1,0:T(8,128)(2,1)S(1)}, bf16[512,256]{1,0:T(8,128)(2,1)S(1)}, u32[]{:S(2)}, u32[]{:S(2)}) collective-permute-start(bf16[512,256]{1,0:T(8,128)(2,1)S(1)} %fusion.8), channel_id=1, source_target_pairs={{0,4},{1,3},{2,6},{3,1},{4,0},{5,7},{6,2},{7,5},{8,12},{9,11},{10,... | collective-permute-start | bytes 786440 | tf_op jit(solution)/shard_map/ppermute | solution.py:42
  108.3 16.7 %collective-permute-start.17 = (bf16[768,256]{1,0:T(8,128)(2,1)S(1)}, bf16[768,256]{1,0:T(8,128)(2,1)S(1)}, u32[]{:S(2)}, u32[]{:S(2)}) collective-permute-start(bf16[768,256]{1,0:T(8,128)(2,1)S(1)} %get-tuple-element.49), channel_id=1, source_target_pairs={{0,2},{1,5},{2,0},{3,7},{4,6},{5,1},{6,4},{7,3},{8,10},{9,13},{10,... | collective-permute-start | bytes 1179656 | tf_op jit(solution)/shard_map/ppermute | solution.py:42
  113.6 19.8 %collective-permute-start.41 = (bf16[768,256]{1,0:T(8,128)(2,1)S(1)}, bf16[768,256]{1,0:T(8,128)(2,1)S(1)}, u32[]{:S(2)}, u32[]{:S(2)}) collective-permute-start(bf16[768,256]{1,0:T(8,128)(2,1)S(1)} %get-tuple-element.51), channel_id=1, source_target_pairs={{0,2},{1,5},{2,0},{3,7},{4,6},{5,1},{6,4},{7,3},{8,10},{9,13},{10,... | collective-permute-start | bytes 1179656 | tf_op jit(solution)/shard_map/ppermute | solution.py:42
  118.6 14.8 %collective-permute-start.19 = (bf16[768,256]{1,0:T(8,128)(2,1)S(1)}, bf16[768,256]{1,0:T(8,128)(2,1)S(1)}, u32[]{:S(2)}, u32[]{:S(2)}) collective-permute-start(bf16[768,256]{1,0:T(8,128)(2,1)S(1)} %fusion.4), channel_id=1, source_target_pairs={{0,4},{1,3},{2,6},{3,1},{4,0},{5,7},{6,2},{7,5},{8,12},{9,11},{10,... | collective-permute-start | bytes 1179656 | tf_op jit(solution)/shard_map/ppermute | solution.py:42
  119.5 15.2 %collective-permute-start.43 = (bf16[768,256]{1,0:T(8,128)(2,1)S(1)}, bf16[768,256]{1,0:T(8,128)(2,1)S(1)}, u32[]{:S(2)}, u32[]{:S(2)}) collective-permute-start(bf16[768,256]{1,0:T(8,128)(2,1)S(1)} %fusion), channel_id=1, source_target_pairs={{0,4},{1,3},{2,6},{3,1},{4,0},{5,7},{6,2},{7,5},{8,12},{9,11},{10,... | collective-permute-start | bytes 1179656 | tf_op jit(solution)/shard_map/ppermute | solution.py:42
  135.3 32.3 %copy-start = (bf16[2048,256]{1,0:T(8,128)(2,1)}, bf16[2048,256]{1,0:T(8,128)(2,1)S(1)}, u32[]{:S(2)}) copy-start(bf16[2048,256]{1,0:T(8,128)(2,1)S(1)} %pad_maximum_fusion.updated_ref) | copy-start | bytes 3145732
  136.5 6.0 %collective-permute-start.44 = (bf16[224,256]{1,0:T(8,128)(2,1)S(1)}, bf16[224,256]{1,0:T(8,128)(2,1)S(1)}, u32[]{:S(2)}, u32[]{:S(2)}) collective-permute-start(bf16[224,256]{1,0:T(8,128)(2,1)S(1)} %broadcast_select_fusion.refs_0_), channel_id=1, source_target_pairs={{0,2},{1,5},{2,0},{3,7},{4,6},{5,1},{6,4},{7,3},{8,10},{9,13},{10,... | collective-permute-start | bytes 344072 | tf_op jit(solution)/shard_map/ppermute | solution.py:42
  137.1 6.2 %collective-permute-start.45 = (bf16[224,256]{1,0:T(8,128)(2,1)S(1)}, bf16[224,256]{1,0:T(8,128)(2,1)S(1)}, u32[]{:S(2)}, u32[]{:S(2)}) collective-permute-start(bf16[224,256]{1,0:T(8,128)(2,1)S(1)} %broadcast_select_fusion.refs_0_), channel_id=1, source_target_pairs={{0,4},{1,3},{2,6},{3,1},{4,0},{5,7},{6,2},{7,5},{8,12},{9,11},{10,... | collective-permute-start | bytes 344072 | tf_op jit(solution)/shard_map/ppermute | solution.py:42
  142.5 4.8 %collective-permute-start.46 = (bf16[224,256]{1,0:T(8,128)(2,1)S(1)}, bf16[224,256]{1,0:T(8,128)(2,1)S(1)}, u32[]{:S(2)}, u32[]{:S(2)}) collective-permute-start(bf16[224,256]{1,0:T(8,128)(2,1)S(1)} %collective-permute-done.44.refs_1_), channel_id=1, source_target_pairs={{0,4},{1,3},{2,6},{3,1},{4,0},{5,7},{6,2},{7,5},{8,12},{9,11},{10,... | collective-permute-start | bytes 344072 | tf_op jit(solution)/shard_map/ppermute | solution.py:42
  142.8 5.2 %collective-permute-start.47 = (bf16[224,256]{1,0:T(8,128)(2,1)S(1)}, bf16[224,256]{1,0:T(8,128)(2,1)S(1)}, u32[]{:S(2)}, u32[]{:S(2)}) collective-permute-start(bf16[224,256]{1,0:T(8,128)(2,1)S(1)} %broadcast_select_fusion.refs_0_), channel_id=1, source_target_pairs={{0,1},{1,0},{2,3},{3,2},{4,5},{5,4},{6,7},{7,6},{8,9},{9,8},{10,11... | collective-permute-start | bytes 344072 | tf_op jit(solution)/shard_map/ppermute | solution.py:42
  142.8 5.2 %collective-permute-start.48 = (bf16[224,256]{1,0:T(8,128)(2,1)S(1)}, bf16[224,256]{1,0:T(8,128)(2,1)S(1)}, u32[]{:S(2)}, u32[]{:S(2)}) collective-permute-start(bf16[224,256]{1,0:T(8,128)(2,1)S(1)} %collective-permute-done.44.refs_1_), channel_id=1, source_target_pairs={{0,1},{1,0},{2,3},{3,2},{4,5},{5,4},{6,7},{7,6},{8,9},{9,8},{10,11... | collective-permute-start | bytes 344072 | tf_op jit(solution)/shard_map/ppermute | solution.py:42
  143.4 4.6 %collective-permute-start.49 = (bf16[224,256]{1,0:T(8,128)(2,1)S(1)}, bf16[224,256]{1,0:T(8,128)(2,1)S(1)}, u32[]{:S(2)}, u32[]{:S(2)}) collective-permute-start(bf16[224,256]{1,0:T(8,128)(2,1)S(1)} %collective-permute-done.45.refs_2_), channel_id=1, source_target_pairs={{0,1},{1,0},{2,3},{3,2},{4,5},{5,4},{6,7},{7,6},{8,9},{9,8},{10,11... | collective-permute-start | bytes 344072 | tf_op jit(solution)/shard_map/ppermute | solution.py:42
  147.3 1.3 collective-permute-start.50
  148.0 22.9 %copy-start.48 = (s32[4]{0:T(128)S(1)}, s32[4]{0:T(128)}, u32[]{:S(2)}) copy-start(s32[4]{0:T(128)} %param.17) | copy-start | bytes 52
  167.6 2.2 %collective-permute-start.51 = (bf16[4,224,256]{2,1,0:T(8,128)(2,1)}, bf16[4,224,256]{2,1,0:T(8,128)(2,1)S(1)}, u32[]{:S(2)}, u32[]{:S(2)}) collective-permute-start(bf16[4,224,256]{2,1,0:T(8,128)(2,1)} %get-tuple-element.48), channel_id=1, source_target_pairs={{0,1},{1,0},{2,3},{3,2},{4,5},{5,4},{6,7},{7,6},{8,9},{9,8},{10,11... | collective-permute-start | bytes 1376264 | tf_op jit(solution)/shard_map/ppermute | solution.py:42
  170.8 4.9 %collective-permute-start.53 = (bf16[224,256]{1,0:T(8,128)(2,1)S(1)}, bf16[224,256]{1,0:T(8,128)(2,1)S(1)}, u32[]{:S(2)}, u32[]{:S(2)}) collective-permute-start(bf16[224,256]{1,0:T(8,128)(2,1)S(1)} %get-tuple-element.63), channel_id=1, source_target_pairs={{0,2},{1,5},{2,0},{3,7},{4,6},{5,1},{6,4},{7,3},{8,10},{9,13},{10,... | collective-permute-start | bytes 344072 | tf_op jit(solution)/shard_map/ppermute | solution.py:42
  171.5 6.8 %collective-permute-start.52 = (bf16[224,256]{1,0:T(8,128)(2,1)S(1)}, bf16[224,256]{1,0:T(8,128)(2,1)S(1)}, u32[]{:S(2)}, u32[]{:S(2)}) collective-permute-start(bf16[224,256]{1,0:T(8,128)(2,1)S(1)} %get-tuple-element.62), channel_id=1, source_target_pairs={{0,2},{1,5},{2,0},{3,7},{4,6},{5,1},{6,4},{7,3},{8,10},{9,13},{10,... | collective-permute-start | bytes 344072 | tf_op jit(solution)/shard_map/ppermute | solution.py:42
  176.6 4.9 %collective-permute-start.54 = (bf16[224,256]{1,0:T(8,128)(2,1)S(1)}, bf16[224,256]{1,0:T(8,128)(2,1)S(1)}, u32[]{:S(2)}, u32[]{:S(2)}) collective-permute-start(bf16[224,256]{1,0:T(8,128)(2,1)S(1)} %fusion.18), channel_id=1, source_target_pairs={{0,4},{1,3},{2,6},{3,1},{4,0},{5,7},{6,2},{7,5},{8,12},{9,11},{10,... | collective-permute-start | bytes 344072 | tf_op jit(solution)/shard_map/ppermute | solution.py:42
  (40 other events, 226.1 us)

commit v2 on v1

v2 whole, which is shorter than its diff:
```python
import functools

import jax
import jax.numpy as jnp
from jax import lax
from jax.experimental import pallas as pl
from jax.experimental.pallas import tpu as pltpu
from jax.sharding import PartitionSpec as P

HD = 64
RADIUS = 127
BLK = 128

epsilon = 1e-06
f32 = jnp.float32
bf16 = jnp.bfloat16

VMEM = pl.BlockSpec(memory_space=pltpu.VMEM)
SMEM = pl.BlockSpec(memory_space=pltpu.SMEM)
ANY = pl.BlockSpec(memory_space=pl.ANY)


def cost(flops):
    return pl.CostEstimate(flops=2 * flops, bytes_accessed=1, transcendentals=0)


def params(mebibytes):
    return pltpu.CompilerParams(vmem_limit_bytes=mebibytes * 1024 * 1024)


class Pairs:
    def __init__(self):
        self.core = [(i, i ^ 1) for i in range(8)]
        self.first = [(i, i ^ (4 if i & 1 else 2)) for i in range(8)]
        self.second = [(i, i ^ (2 if i & 1 else 4)) for i in range(8)]

    def places(self, width):
        offsets = self.offsets(width)
        return jnp.concatenate([offsets, offsets[:3], offsets[6:7], offsets[3:6], offsets[7:]])

    def offsets(self, width):
        me = lax.axis_index("tp")
        first = jnp.where(me & 1 == 1, 4, 2)
        second = 6 - first
        blocks = [0, first, second, 1, 1 ^ second, 1 ^ first, 6, 7]
        return jnp.stack([(me ^ block) * width for block in blocks]).astype(jnp.int32)


def move(value, pairs):
    return lax.ppermute(value, "tp", pairs)


def gather_blocks(pairs, own, chunks):
    first = move(own, pairs.first)
    second = move(own, pairs.second)
    same_chip = [own, first, second]
    whole = same_chip + [move(block, pairs.core) for block in same_chip]
    across = [move(rows_of(first, chunk), pairs.second) for chunk in chunks]
    return whole, [[block, move(block, pairs.core)] for block in across]


def gather_few(pairs, own):
    first = move(own, pairs.first)
    second = move(own, pairs.second)
    across = move(first, pairs.second)
    same_chip = [own, first, second, across]
    cores = [move(block, pairs.core) for block in same_chip]
    return same_chip[:3] + cores[:3] + [across, cores[3]]


def rows_of(array, blocks):
    pieces = [array[start : start + rows] for start, rows, _ in runs_of(blocks)]
    return pieces[0] if len(pieces) == 1 else jnp.concatenate(pieces, axis=0)


def runs_of(blocks):
    runs, start = [], 0
    for at in range(1, len(blocks) + 1):
        if at == len(blocks) or blocks[at] != blocks[at - 1] + 1:
            runs.append((blocks[start] * BLK, (at - start) * BLK, start * BLK))
            start = at
    return runs


def add(left, right):
    return left.astype(f32) + right.astype(f32)


def reduce_blocks(pairs, keep, send):
    other = move(send, pairs.core)
    across = move(add(keep[3], other[3]).astype(bf16), pairs.first)
    near = move(add(keep[1], other[1]).astype(bf16), pairs.first)
    turned = (add(keep[2], other[2]) + across.astype(f32)).astype(bf16)
    far = move(turned, pairs.second)
    return [keep, other, near, far], [other, across, far]


def total(terms):
    wide = [(term[0] if term.ndim == 3 else term).astype(f32) for term in terms]
    return functools.reduce(lambda left, right: left + right, wide)


def row_scale(blocks, features):
    total = None
    for block in blocks:
        wide = block.astype(f32)
        total = wide * wide if total is None else total + wide * wide
    return lax.rsqrt(jnp.sum(total, axis=-1, keepdims=True) / features + epsilon)


def columns_of(count, width, offsets, number):
    if count == 1:
        return slice(None)
    return pl.ds(pl.multiple_of(offsets[number], width), width)


def qkv_kernel(count, runs, offsets, gain_ref, weight_ref, *refs):
    blocks, (query_ref, pair_ref, gained) = refs[:count], refs[-3:]
    rows, features = gained.shape
    width = blocks[0].shape[1]
    scales = []
    for first, amount, place in runs:
        values = []
        for block in blocks:
            start = place if block.shape[0] == rows else first
            values.append(block[start : start + amount, :])
        for number, value in enumerate(values):
            columns = columns_of(count, width, offsets, number)
            gained[place : place + amount, columns] = value * (gain_ref[:, columns] * 0.0625)
        scales.append(row_scale(values, features) * 16.0)
    scale = scales[0] if len(scales) == 1 else jnp.concatenate(scales, axis=0)
    query = jnp.dot(gained[...], weight_ref[0], preferred_element_type=f32)
    query_ref[...] = (query * (scale * (1.0 / HD**0.5))).astype(bf16)
    local_width = query_ref.shape[1]
    for number in range(2):
        value = jnp.dot(gained[...], weight_ref[1 + number], preferred_element_type=f32)
        pair_ref[:, number * local_width : (number + 1) * local_width] = (value * scale).astype(bf16)


def qkv(blocks, runs, offsets, gain_row, attn_in, after):
    rows = sum(amount for _, amount, _ in runs)
    features, local_width = attn_in.shape[1:]
    count = len(blocks)
    return pl.pallas_call(
        functools.partial(qkv_kernel, count, runs),
        out_shape=[
            jax.ShapeDtypeStruct((rows, local_width), bf16),
            jax.ShapeDtypeStruct((rows, 2 * local_width), bf16),
        ],
        in_specs=[SMEM, VMEM, VMEM] + [VMEM] * count + [ANY] * len(after),
        out_specs=[VMEM] * 2,
        scratch_shapes=[pltpu.VMEM((rows, features), bf16)],
        compiler_params=params(12),
        cost_estimate=cost(2 * rows * features * 3 * local_width),
        name="norm_qkv",
    )(offsets, gain_row, attn_in, *blocks, *after)


def project(rows_ref, weight_ref, offsets, outs):
    if len(outs) == 1:
        outs[0][...] = jnp.dot(rows_ref[...], weight_ref[...], preferred_element_type=f32).astype(bf16)
        return
    width = outs[0].shape[2]
    for side, out in enumerate(outs):
        for number in range(4):
            columns = pl.ds(pl.multiple_of(offsets[8 + 4 * side + number], width), width)
            value = jnp.dot(rows_ref[...], weight_ref[:, columns], preferred_element_type=f32)
            out[number] = value.astype(bf16)


def partial_shapes(split, rows, features, width):
    if split:
        return [jax.ShapeDtypeStruct((4, rows, width), bf16)] * 2
    return [jax.ShapeDtypeStruct((rows, features), bf16)]


def stack_heads(query, head_of, heads):
    return jnp.concatenate(
        [jnp.where(head_of == head, query, jnp.zeros_like(query)) for head in range(heads)], axis=0
    )


def pick_heads(mixed, head_of):
    chosen = mixed[0]
    for head in range(1, mixed.shape[0]):
        chosen = jnp.where(head_of == head, mixed[head], chosen)
    return chosen.astype(bf16)


def attention_kernel(queries, keys, n_arrays, n_outs, ends, offsets, weight_ref, *refs):
    arrays, outs, context = refs[:n_arrays], refs[-1 - n_outs : -1], refs[-1]
    width = weight_ref.shape[0]
    heads = width // HD
    span = 3 * BLK
    row = lax.broadcasted_iota(jnp.int32, (BLK, span), 0)
    column = lax.broadcasted_iota(jnp.int32, (BLK, span), 1)
    band = (column - row >= BLK - RADIUS) & (column - row <= BLK + RADIUS)
    head_of = lax.broadcasted_iota(jnp.int32, (BLK, width), 1) // HD

    def load(kind, block):
        number, start = keys[block]
        if kind == 0:
            return arrays[2 * number][start : start + BLK, :]
        return arrays[2 * number + 1][start : start + BLK, (kind - 1) * width : kind * width]

    for place, block in enumerate(queries):
        stacked = stack_heads(load(0, block), head_of, heads)
        key = jnp.concatenate([load(1, block + step) for step in (-1, 0, 1)], axis=0)
        value = jnp.concatenate([load(2, block + step) for step in (-1, 0, 1)], axis=0)
        scores = lax.dot_general(stacked, key, (((1,), (1,)), ((), ())), preferred_element_type=f32)
        usable = band
        if keys[block - 1] is keys["low"]:
            usable = usable & ((column >= BLK) | (ends[0] > 0))
        if keys[block + 1] is keys["high"]:
            usable = usable & ((column < 2 * BLK) | (ends[1] > 0))
        scores = jnp.where(usable[None], scores.reshape(heads, BLK, span), -jnp.inf)
        top = jnp.max(scores, axis=-1, keepdims=True)
        expo = jnp.exp(scores - top)
        share = 1.0 / jnp.sum(expo, axis=-1, keepdims=True)
        expo = expo.astype(bf16).reshape(heads * BLK, span)
        mixed = jnp.dot(expo, value, preferred_element_type=f32).reshape(heads, BLK, width) * share
        context[place * BLK : (place + 1) * BLK, :] = pick_heads(mixed, head_of)
    project(context, weight_ref, offsets, outs)


def attention(queries, keys, arrays, ends, offsets, attn_out, split, after):
    rows = len(queries) * BLK
    width, features = attn_out.shape
    flat = [piece for pair in arrays for piece in pair]
    outs = partial_shapes(split, rows, features, width)
    heads = width // HD
    return pl.pallas_call(
        functools.partial(attention_kernel, queries, keys, len(flat), len(outs)),
        out_shape=outs,
        in_specs=[SMEM, SMEM, VMEM] + [VMEM] * len(flat) + [ANY] * len(after),
        out_specs=[VMEM] * len(outs),
        scratch_shapes=[pltpu.VMEM((rows, width), bf16)],
        compiler_params=params(12),
        cost_estimate=cost(2 * rows * (2 * 3 * BLK * width * heads + width * features)),
        name="band_attention",
    )(ends, offsets, attn_out, *flat, *after)


def routed_kernel(places, n_outs, origin, ends, offsets, rows_ref, weight_ref, *refs):
    count = len(places)
    arrays = [refs[2 * number : 2 * number + 2] for number in range(count)]
    outs, (scores, context) = refs[-2 - n_outs : -2], refs[-2:]
    slots, width = context.shape
    heads = width // HD
    wanted = rows_ref[...]
    head_of = lax.broadcasted_iota(jnp.int32, (slots, width), 1) // HD

    def positions(number):
        column = lax.broadcasted_iota(jnp.int32, (1, arrays[number][1].shape[0]), 1)
        position = column
        for start, _, first in places[number]:
            position = jnp.where(column >= first, column - first + start, position)
        return position

    query = None
    for number in range(origin):
        one_hot = (positions(number) == wanted).astype(f32).astype(bf16)
        part = jnp.dot(one_hot, arrays[number][0][...], preferred_element_type=f32)
        query = part if query is None else query + part
    stacked = stack_heads(query.astype(bf16), head_of, heads)
    top, starts = None, []
    for number in range(count):
        starts.append(starts[-1] + arrays[number - 1][1].shape[0] if number else 0)
        key = arrays[number][1][:, :width]
        far = positions(number) - wanted
        usable = (far <= RADIUS) & (far >= -RADIUS)
        if number >= origin:
            usable = usable & (ends[number - origin] > 0)
        piece = lax.dot_general(stacked, key, (((1,), (1,)), ((), ())), preferred_element_type=f32)
        piece = jnp.where(usable[None], piece.reshape(heads, slots, key.shape[0]), -jnp.inf)
        scores[:, :, starts[number] : starts[number] + key.shape[0]] = piece
        high = jnp.max(piece, axis=-1, keepdims=True)
        top = high if top is None else jnp.maximum(top, high)
    total, mixed = None, None
    for number in range(count):
        value = arrays[number][1][:, width:]
        expo = jnp.exp(scores[:, :, starts[number] : starts[number] + value.shape[0]] - top)
        amount = jnp.sum(expo, axis=-1, keepdims=True)
        expo = expo.astype(bf16).reshape(heads * slots, value.shape[0])
        part = jnp.dot(expo, value, preferred_element_type=f32)
        total = amount if total is None else total + amount
        mixed = part if mixed is None else mixed + part
    mixed = mixed.reshape(heads, slots, width) * (1.0 / total)
    context[...] = pick_heads(mixed, head_of)
    project(context, weight_ref, offsets, outs)


def routed_attention(places, arrays, ends, offsets, route_rows, attn_out, split, origin):
    slots = route_rows.shape[1]
    width, features = attn_out.shape
    flat = [piece for pair in arrays for piece in pair]
    outs = partial_shapes(split, slots, features, width)
    heads = width // HD
    span = sum(pair[1].shape[0] for pair in arrays)
    return pl.pallas_call(
        functools.partial(routed_kernel, places, len(outs), origin),
        out_shape=outs,
        in_specs=[SMEM, SMEM, VMEM, VMEM] + [VMEM] * len(flat),
        out_specs=[VMEM] * len(outs),
        scratch_shapes=[pltpu.VMEM((heads, slots, span), f32), pltpu.VMEM((slots, width), bf16)],
        compiler_params=params(20),
        cost_estimate=cost(2 * slots * (2 * span * width * heads + width * features)),
        name="routed_attention",
    )(ends, offsets, route_rows.reshape(slots, 1), attn_out, *flat)


def ffn_kernel(count, n_outs, tile, offsets, gain_ref, in_ref, down_hbm, *refs):
    blocks, outs = refs[:count], refs[-6 - n_outs : -6]
    normed, hidden, gate_ref, up_ref, down_ref, semaphores = refs[-6:]
    features, width = normed.shape[1], blocks[0].shape[1]
    tiles = [slice(start, start + tile) for start in range(0, hidden.shape[1], tile)]
    copies = []

    def start(source, target):
        copies.append(pltpu.make_async_copy(source, target, semaphores.at[len(copies)]))
        copies[-1].start()

    for columns in tiles:
        start(in_ref.at[0, :, columns], gate_ref.at[:, columns])
        start(in_ref.at[1, :, columns], up_ref.at[:, columns])
    if n_outs == 1:
        start(down_hbm, down_ref)
    else:
        for number in range(8):
            columns = pl.ds(pl.multiple_of(offsets[8 + number], width), width)
            start(down_hbm.at[:, columns], down_ref.at[:, number * width : (number + 1) * width])
    values = [block[...] for block in blocks]
    scale = row_scale(values, features)
    for number, value in enumerate(values):
        columns = columns_of(count, width, offsets, number)
        value = value.astype(f32) * scale * gain_ref[:, columns].astype(f32)
        normed[:, columns] = value.astype(bf16)
    for number, columns in enumerate(tiles):
        copies[2 * number].wait()
        gate = jnp.dot(normed[...], gate_ref[:, columns], preferred_element_type=f32)
        copies[2 * number + 1].wait()
        up = jnp.dot(normed[...], up_ref[:, columns], preferred_element_type=f32)
        hidden[:, columns] = (jax.nn.gelu(gate, approximate=True) * up).astype(bf16)
    if n_outs == 1:
        copies[-1].wait()
        outs[0][...] = jnp.dot(hidden[...], down_ref[...], preferred_element_type=f32).astype(bf16)
    else:
        for number in range(8):
            copies[2 * len(tiles) + number].wait()
            weight = down_ref[:, number * width : (number + 1) * width]
            value = jnp.dot(hidden[...], weight, preferred_element_type=f32)
            outs[number // 4][number % 4] = value.astype(bf16)


def ffn(blocks, offsets, gain_row, ffn_in, ffn_out, split, after):
    rows, width = blocks[0].shape
    hidden, features = ffn_out.shape
    count = len(blocks)
    tile = 512 if hidden % 512 == 0 else 128
    outs = partial_shapes(split, rows, features, width)
    return pl.pallas_call(
        functools.partial(ffn_kernel, count, len(outs), tile),
        out_shape=outs,
        in_specs=[SMEM, VMEM, ANY, ANY] + [VMEM] * count + [ANY] * len(after),
        out_specs=[VMEM] * len(outs),
        scratch_shapes=[
            pltpu.VMEM((rows, features), bf16),
            pltpu.VMEM((rows, hidden), bf16),
            pltpu.VMEM((features, hidden), bf16),
            pltpu.VMEM((features, hidden), bf16),
            pltpu.VMEM((hidden, features), bf16),
            pltpu.SemaphoreType.DMA((2 * hidden // tile + 8,)),
        ],
        compiler_params=params(38),
        cost_estimate=cost(2 * rows * features * 3 * hidden),
        name="heavy_ffn",
    )(
        offsets,
        gain_row,
        pltpu.with_memory_space_constraint(ffn_in, pltpu.HBM),
        pltpu.with_memory_space_constraint(ffn_out, pltpu.HBM),
        *blocks,
        *after,
    )


def total_of(refs):
    total = None
    for ref in refs:
        wide = (ref[...] if len(ref.shape) == 2 else ref[0]).astype(f32)
        total = wide if total is None else total + wide
    return total


def spread_kernel(groups, rows_ref, used_ref, *refs):
    pieces, terms, out_ref = refs[: len(groups)], refs[len(groups) : -1], refs[-1]
    slots = rows_ref.shape[1]
    heavy = jnp.where(used_ref[...] > 0, total_of(terms), 0.0)
    coarse = heavy.astype(bf16)
    fine = (heavy - coarse.astype(f32)).astype(bf16)
    for (start, rows), piece in zip(groups, pieces):
        position = lax.broadcasted_iota(jnp.int32, (rows, slots), 0) + start
        one_hot = (position == rows_ref[...]).astype(f32).astype(bf16)
        extra = jnp.dot(one_hot, coarse, preferred_element_type=f32)
        extra += jnp.dot(one_hot, fine, preferred_element_type=f32)
        out_ref[start : start + rows, :] = (piece[...].astype(f32) + extra).astype(bf16)


def spread(groups, pieces, terms, route_rows, usable_slots):
    rows, width = sum(rows for _, rows in groups), pieces[0].shape[1]
    return pl.pallas_call(
        functools.partial(spread_kernel, groups),
        out_shape=jax.ShapeDtypeStruct((rows, width), bf16),
        in_specs=[VMEM] * (2 + len(pieces) + len(terms)),
        out_specs=VMEM,
        compiler_params=params(12),
        name="spread_rows",
    )(route_rows, usable_slots.astype(jnp.int32)[:, None], *pieces, *terms)


def plan(total):
    middle = total // 2
    chunks = [[0, 1, total - 2, total - 1], list(range(2, middle)), list(range(middle, total - 2))]
    return chunks, [list(range(middle)), list(range(middle, total))]


def local(
    residual, attn_gain, attn_in, attn_out, ffn_gain, ffn_in, ffn_out, route_rows, route_counts
):
    seq_count = lax.axis_size("seq")
    seq_index = lax.axis_index("seq")
    tok_rows, width = residual.shape
    split = lax.axis_size("tp") == 8
    chunks, groups = plan(tok_rows // BLK)
    if split:
        pairs = Pairs()
        offsets = pairs.places(width)
        gather = functools.partial(gather_few, pairs)
        reduce = functools.partial(reduce_blocks, pairs)
        whole, late = gather_blocks(pairs, residual, chunks)
    else:
        offsets = jnp.zeros((1,), jnp.int32)

        def gather(own):
            return [lax.all_gather(own, "tp", axis=1, tiled=True)]

        def reduce(part):
            total = lax.psum_scatter(part, "tp", scatter_dimension=1, tiled=True)
            return [total], [total]

        whole, late = gather(residual), [[]] * len(chunks)

    ends = jnp.stack([seq_index > 0, seq_index < seq_count - 1]).astype(jnp.int32)
    keys, arrays, places = {}, [], []
    low = high = None
    for number, blocks in enumerate(chunks):
        after = [arrays[-1][0]] if arrays else []
        runs = runs_of(blocks)
        query, pair = qkv(whole + late[number], runs, offsets, attn_gain[None], attn_in, after)
        for at, block in enumerate(blocks):
            keys[block] = (len(arrays), at * BLK)
        arrays.append([query, pair])
        places.append(runs)
        if number == 0:
            up = [(i, i + 1) for i in range(seq_count - 1)]
            down = [(target, source) for source, target in up]
            low = lax.ppermute(pair[-BLK:], "seq", up)
            high = lax.ppermute(pair[:BLK], "seq", down)
    origin = len(arrays)
    keys["low"] = keys[-1] = (origin, 0)
    keys["high"] = keys[tok_rows // BLK] = (origin + 1, 0)
    arrays += [[low, low], [high, high]]
    places += [[(-BLK, BLK, 0)], [(tok_rows, BLK, 0)]]

    routed = routed_attention(places, arrays, ends, offsets, route_rows, attn_out, split, origin)
    mixed, _ = reduce(*routed)
    taken = (jnp.take(residual, route_rows[0], axis=0).astype(f32) + total(mixed)).astype(bf16)

    spans, pieces, previous, moves = [], [], routed[0], []
    for number, queries in enumerate(groups):
        needed = sorted({keys[b + step][0] for b in queries for step in (-1, 0, 1)})
        place = {array: at for at, array in enumerate(needed)}
        inner = {name: (place.get(array), start) for name, (array, start) in keys.items()}
        inner["low"] = inner[-1]
        inner["high"] = inner[tok_rows // BLK]
        used = [arrays[array] for array in needed]
        parts = attention(queries, inner, used, ends, offsets, attn_out, split, [previous])
        previous = parts[0]
        terms, moved = reduce(*parts)
        moves.append(moved)
        spans.append((queries[0] * BLK, len(queries) * BLK))
        pieces.append((rows_of(residual, queries).astype(f32) + total(terms)).astype(bf16))

    slots = jnp.arange(route_rows.shape[1], dtype=jnp.int32)
    row_count = lax.dynamic_index_in_dim(route_counts, seq_index, 0, keepdims=False)
    parts = ffn(gather(taken), offsets, ffn_gain[None], ffn_in, ffn_out, split, moves[0][1:2])
    terms, _ = reduce(*parts)
    return spread(spans, pieces, terms, route_rows, slots < row_count)


def solution(mesh):
    in_specs = (
        P("seq", "tp"),
        P(),
        P(None, None, "tp"),
        P("tp", None),
        P(),
        P(None, None, "tp"),
        P("tp", None),
        P("seq", None),
        P(),
    )
    out_specs = P("seq", "tp")
    return jax.shard_map(local, mesh=mesh, in_specs=in_specs, out_specs=out_specs, check_vma=False)
```

time: 188 us -> 165 us (0.88)
  Pallas kernels: 65.6 us -> 52.2 us
  starting transfers between devices: 45.5 us -> 32.7 us
  other arithmetic: 8.33 us -> 12.6 us
  local copies, waits for them, and re-layouts: 10.8 us -> 8.34 us
  waiting for transfers between devices: 56.4 us -> 58.6 us
    ppermute x51 -> x34, starting transfers between devices: 34.9 us -> 26.7 us  [move(): return lax.ppermute(value, 'tp', pairs)]
    pallas_call x6, Pallas kernels: 47.7 us -> 40.2 us  [the longest x1 15.6 us: ffn(): pl.pallas_call(functools.partial(ffn_kernel, count, len(outs), tile), out...]
    pallas_call x3 -> x2, Pallas kernels: 18 us -> 12 us  [attention(): pl.pallas_call(functools.partial(attention_kernel, queries, keys, len(fla...]
    ppermute x4 -> x2, starting transfers between devices: 10.6 us -> 6.03 us  [the longest x1 4.73 us: local(): low = lax.ppermute(pair[-BLK:], 'seq', up)]
    convert_element_type x4 -> x3, other arithmetic: 2.56 us -> 5.33 us  [reduce_blocks(): near = move(add(keep[1], other[1]).astype(bf16), pairs.first)]
    ppermute x51 -> x34, waiting for transfers between devices: 56 us -> 58.6 us  [move(): return lax.ppermute(value, 'tp', pairs)]
    convert_element_type x4, other arithmetic: 1.34 us -> 3.67 us  [reduce_blocks(): turned = (add(keep[2], other[2]) + across.astype(f32)).astype(bf16)]
    convert_element_type x2 -> x3, other arithmetic: 0.71 us -> 2.96 us  [the longest x1 1.84 us: local(): (rows_of(residual, queries).astype(f32) + total(terms)).astype(bf16)]
  transfers between devices with their start and end apart: 55 -> 36, of which waited for: 20 -> 10; matrix products, arithmetic and copies ran while one was open for 5% -> 9% of each run, Pallas kernels for 23% -> 22%
where the time goes in v2:
time: 165 us
  waiting for transfers between devices  58.6 us (36%)
  Pallas kernels  52.2 us (32%)
  starting transfers between devices  32.7 us (20%)
  other arithmetic  12.6 us (8%)
  local copies, waits for them, and re-layouts  8.34 us (5%)
    ppermute x34, waiting for transfers between devices, move(): return lax.ppermute(value, 'tp', pairs)  58.6 us
    ppermute x34, starting transfers between devices, move(): return lax.ppermute(value, 'tp', pairs)  26.7 us
    pallas_call x1, Pallas kernels, ffn(): pl.pallas_call(functools.partial(ffn_kernel, count, len(outs), tile), out...  15.6 us
    pallas_call x3, Pallas kernels, qkv(): pl.pallas_call(functools.partial(qkv_kernel, count, runs), out_shape=[jax...  15.1 us
    pallas_call x2, Pallas kernels, attention(): pl.pallas_call(functools.partial(attention_kernel, queries, keys, len(fla...  12 us
    pallas_call x1, Pallas kernels, routed_attention(): pl.pallas_call(functools.partial(routed_kernel, places, len(outs), origin...  7.7 us
    unnamed x26, local copies, waits for them, and re-layouts  5.48 us
    convert_element_type x3, other arithmetic, reduce_blocks(): near = move(add(keep[1], other[1]).astype(bf16), pairs.first)  5.33 us
  transfers between devices with their start and end apart: 36, of which 10 were waited for; matrix products, arithmetic and copies ran while one was open for 9% of the time, Pallas kernels for 22%

profile of v2, /device:TPU:0, one launch (start us, length us, event | category | flops | bytes accessed | tf_op | source)
XLA Modules:
  0.0 164.8 jit_solution(18427039824578500168)
XLA Ops:
  0.0 3.0 %collective-permute-start.1 = (bf16[2048,256]{1,0:T(8,128)(2,1)}, bf16[2048,256]{1,0:T(8,128)(2,1)}, u32[]{:S(2)}, u32[]{:S(2)}) collective-permute-start(bf16[2048,256]{1,0:T(8,128)(2,1)} %refs_0_.5), channel_id=1, source_target_pairs={{0,4},{1,3},{2,6},{3,1},{4,0},{5,7},{6,2},{7,5},{8,12},{9,11},{10,... | collective-permute-start | bytes 3145736 | tf_op jit(solution)/shard_map/ppermute | solution.py:50
  3.0 1.5 collective-permute-start
  4.5 22.3 %collective-permute-done.1.refs_2_ = bf16[2048,256]{1,0:T(8,128)(2,1)} collective-permute-done((bf16[2048,256]{1,0:T(8,128)(2,1)}, bf16[2048,256]{1,0:T(8,128)(2,1)}, u32[]{:S(2)}, u32[]{:S(2)}) %collective-permute-start.1) | collective-permute-done | bytes 1048608 | tf_op jit(solution)/shard_map/ppermute | solution.py:50
  26.9 0.5 collective-permute-start.3
  27.4 2.5 %collective-permute-start.5 = (bf16[512,256]{1,0:T(8,128)(2,1)S(1)}, bf16[512,256]{1,0:T(8,128)(2,1)S(1)}, u32[]{:S(2)}, u32[]{:S(2)}) collective-permute-start(bf16[512,256]{1,0:T(8,128)(2,1)S(1)} %pad_maximum_fusion), channel_id=1, source_target_pairs={{0,4},{1,3},{2,6},{3,1},{4,0},{5,7},{6,2},{7,5},{8,12},{9,11},{10,... | collective-permute-start | bytes 786440 | tf_op jit(solution)/shard_map/ppermute | solution.py:50
  29.9 0.9 fusion.22
  30.9 1.0 copy-done.7
  31.9 2.0 %collective-permute-start.7 = (bf16[768,256]{1,0:T(8,128)(2,1)}, bf16[768,256]{1,0:T(8,128)(2,1)S(1)}, u32[]{:S(2)}, u32[]{:S(2)}) collective-permute-start(bf16[768,256]{1,0:T(8,128)(2,1)} %get-tuple-element.40), channel_id=1, source_target_pairs={{0,4},{1,3},{2,6},{3,1},{4,0},{5,7},{6,2},{7,5},{8,12},{9,11},{10,... | collective-permute-start | bytes 1179656 | tf_op jit(solution)/shard_map/ppermute | solution.py:50
  33.9 0.4 collective-permute-done.5.refs_6_
  34.3 0.1 copy.10.rows_ref
  34.5 0.1 concatenate.10.offsets
  34.6 0.1 add_convert_fusion.8.ends
  34.6 4.3 %collective-permute-done.9.refs_6_ = bf16[768,256]{1,0:T(8,128)(2,1)} collective-permute-done((bf16[768,256]{1,0:T(8,128)(2,1)}, bf16[768,256]{1,0:T(8,128)(2,1)}, u32[]{:S(2)}, u32[]{:S(2)}) %collective-permute-start.9) | collective-permute-done | bytes 393248 | tf_op jit(solution)/shard_map/ppermute | solution.py:50
  39.0 4.1 %collective-permute-done.7.refs_6_ = bf16[768,256]{1,0:T(8,128)(2,1)S(1)} collective-permute-done((bf16[768,256]{1,0:T(8,128)(2,1)}, bf16[768,256]{1,0:T(8,128)(2,1)S(1)}, u32[]{:S(2)}, u32[]{:S(2)}) %collective-permute-start.7) | collective-permute-done | bytes 393248 | tf_op jit(solution)/shard_map/ppermute | solution.py:50
  43.1 1.9 %copy-done.5 = bf16[3,2048,256]{2,1,0:T(8,128)(2,1)S(1)} copy-done((bf16[3,2048,256]{2,1,0:T(8,128)(2,1)S(1)}, bf16[3,2048,256]{2,1,0:T(8,128)(2,1)}, u32[]{:S(2)}) %copy-start.5) | copy-done | bytes 3145752
  45.0 1.2 copy-done.8
  46.2 4.3 %norm_qkv.3 = (bf16[512,256]{1,0:T(8,128)(2,1)S(1)}, bf16[512,512]{1,0:T(8,128)(2,1)S(1)}) custom-call(s32[16]{0:T(128)S(1)} %concatenate.10.offsets, bf16[1,2048]{1,0:T(2,128)(2,1)S(1)} %broadcast_in_dim.19.gain_ref, bf16[3,2048,256]{2,1,0:T(8,128)(2,1)S(1)} %copy-done.5, bf16[2048,256]{1,0:T(8,128)(2,1)S(1)} %copy-done, ...), custom_call_target="tpu_custom_call" | custom-call | flops 3221225472 | bytes 1 | tf_op jit(solution)/shard_map/norm_qkv/pallas_call | solution.py:144
  50.5 1.3 collective-permute-start.12
  51.8 4.7 %collective-permute-start.11 = (bf16[128,512]{1,0:T(8,128)(2,1)S(1)}, bf16[128,512]{1,0:T(8,128)(2,1)S(1)}, u32[]{:S(2)}, u32[]{:S(2)}) collective-permute-start(bf16[128,512]{1,0:T(8,128)(2,1)S(1)} %get-tuple-element.48), channel_id=1, source_target_pairs={{0,8},{8,16},{16,24},{1,9},{9,17},{17,25},{2,10},{10,18},{18,26},{... | collective-permute-start | bytes 393224 | tf_op jit(solution)/shard_map/ppermute | solution.py:467
  56.6 5.4 %norm_qkv.4 = (bf16[768,256]{1,0:T(8,128)(2,1)S(1)}, bf16[768,512]{1,0:T(8,128)(2,1)S(1)}) custom-call(s32[16]{0:T(128)S(1)} %concatenate.10.offsets, bf16[1,2048]{1,0:T(2,128)(2,1)S(1)} %broadcast_in_dim.19.gain_ref, bf16[3,2048,256]{2,1,0:T(8,128)(2,1)S(1)} %copy-done.5, bf16[2048,256]{1,0:T(8,128)(2,1)S(1)} %copy-done, ...), custom_call_target="tpu_custom_call" | custom-call | flops 4831838208 | bytes 1 | tf_op jit(solution)/shard_map/norm_qkv/pallas_call | solution.py:144
  61.9 5.5 %norm_qkv.5 = (bf16[768,256]{1,0:T(8,128)(2,1)S(1)}, bf16[768,512]{1,0:T(8,128)(2,1)S(1)}) custom-call(s32[16]{0:T(128)S(1)} %concatenate.10.offsets, bf16[1,2048]{1,0:T(2,128)(2,1)S(1)} %broadcast_in_dim.19.gain_ref, bf16[3,2048,256]{2,1,0:T(8,128)(2,1)S(1)} %copy-done.5, bf16[2048,256]{1,0:T(8,128)(2,1)S(1)} %copy-done, ...), custom_call_target="tpu_custom_call" | custom-call | flops 4831838208 | bytes 1 | tf_op jit(solution)/shard_map/norm_qkv/pallas_call | solution.py:144
  67.5 7.7 %routed_attention.1 = (bf16[4,224,256]{2,1,0:T(8,128)(2,1)S(1)}, bf16[4,224,256]{2,1,0:T(8,128)(2,1)}) custom-call(s32[2]{0:T(128)S(1)} %add_convert_fusion.8.ends, s32[16]{0:T(128)S(1)} %concatenate.10.offsets, s32[224,1]{1,0:T(8,128)S(1)} %copy.10.rows_ref, bf16[256,2048]{1,0:T(8,128)(2,1)S(1)} %copy-done.6, ...), custom_call_target="tpu_custom_call" | custom-call | flops 4697620480 | bytes 1 | tf_op jit(solution)/shard_map/routed_attention/pallas_call | solution.py:300
  75.2 6.1 %band_attention.2 = (bf16[4,1024,256]{2,1,0:T(8,128)(2,1)S(1)}, bf16[4,1024,256]{2,1,0:T(8,128)(2,1)}) custom-call(s32[2]{0:T(128)S(1)} %add_convert_fusion.8.ends, s32[16]{0:T(128)S(1)} %concatenate.10.offsets, bf16[256,2048]{1,0:T(8,128)(2,1)S(1)} %copy-done.6, bf16[512,256]{1,0:T(8,128)(2,1)S(1)} %get-tuple-element.19.refs_8_.refs_0_, ...), custom_call_target="tpu_custom_call" | custom-call | flops 5368709120 | bytes 1 | tf_op jit(solution)/shard_map/band_attention/pallas_call | solution.py:232
  81.3 5.9 %band_attention.3 = (bf16[4,1024,256]{2,1,0:T(8,128)(2,1)S(1)}, bf16[4,1024,256]{2,1,0:T(8,128)(2,1)}) custom-call(s32[2]{0:T(128)S(1)} %add_convert_fusion.8.ends, s32[16]{0:T(128)S(1)} %concatenate.10.offsets, bf16[256,2048]{1,0:T(8,128)(2,1)S(1)} %copy-done.6, bf16[512,256]{1,0:T(8,128)(2,1)S(1)} %get-tuple-element.19.refs_8_.refs_0_, ...), custom_call_target="tpu_custom_call" | custom-call | flops 5368709120 | bytes 1 | tf_op jit(solution)/shard_map/band_attention/pallas_call | solution.py:232
  87.2 1.4 copy-done.1
  88.5 0.5 collective-permute-start.17
  89.1 1.1 gather_fusion
  90.1 3.7 %collective-permute-done.21 = bf16[4,224,256]{2,1,0:T(8,128)(2,1)} collective-permute-done((bf16[4,224,256]{2,1,0:T(8,128)(2,1)}, bf16[4,224,256]{2,1,0:T(8,128)(2,1)}, u32[]{:S(2)}, u32[]{:S(2)}) %collective-permute-start.21) | collective-permute-done | bytes 458784 | tf_op jit(solution)/shard_map/ppermute | solution.py:50
  93.8 1.1 fusion.17
  95.0 0.7 collective-permute-start.23
  95.7 1.4 collective-permute-start.22
  97.1 2.7 %collective-permute-done.23 = bf16[224,256]{1,0:T(8,128)(2,1)S(1)} collective-permute-done((bf16[224,256]{1,0:T(8,128)(2,1)S(1)}, bf16[224,256]{1,0:T(8,128)(2,1)S(1)}, u32[]{:S(2)}, u32[]{:S(2)}) %collective-permute-start.23) | collective-permute-done | bytes 114720 | tf_op jit(solution)/shard_map/ppermute | solution.py:50
  99.8 1.0 fusion.13
  100.8 1.7 %collective-permute-start.24 = (bf16[224,256]{1,0:T(8,128)(2,1)S(1)}, bf16[224,256]{1,0:T(8,128)(2,1)S(1)}, u32[]{:S(2)}, u32[]{:S(2)}) collective-permute-start(bf16[224,256]{1,0:T(8,128)(2,1)S(1)} %fusion.13), channel_id=1, source_target_pairs={{0,4},{1,3},{2,6},{3,1},{4,0},{5,7},{6,2},{7,5},{8,12},{9,11},{10,... | collective-permute-start | bytes 344072 | tf_op jit(solution)/shard_map/ppermute | solution.py:50
  102.6 2.4 %fusion.8 = (bf16[1024,256]{1,0:T(8,128)(2,1)}, bf16[1024,256]{1,0:T(8,128)(2,1)}) fusion(bf16[4,1024,256]{2,1,0:T(8,128)(2,1)} %collective-permute-done.13, bf16[4,1024,256]{2,1,0:T(8,128)(2,1)S(1)} %get-tuple-element.26.refs_8_), kind=kLoop, calls=%fused_computation.17 | loop fusion | flops 2097152 | bytes 3145728 | tf_op jit(solution)/shard_map/convert_element_type | solution.py:92
  105.0 0.7 collective-permute-start.15
  105.7 1.1 fusion.16.refs_0_
  106.7 1.4 collective-permute-start.25
  108.2 1.0 collective-permute-start.26
  109.2 7.7 %collective-permute-done.25.refs_1_ = bf16[224,256]{1,0:T(8,128)(2,1)S(1)} collective-permute-done((bf16[224,256]{1,0:T(8,128)(2,1)S(1)}, bf16[224,256]{1,0:T(8,128)(2,1)S(1)}, u32[]{:S(2)}, u32[]{:S(2)}) %collective-permute-start.25) | collective-permute-done | bytes 114720 | tf_op jit(solution)/shard_map/ppermute | solution.py:50
  116.8 0.4 collective-permute-start.30
  117.2 0.6 dynamic_slice.4
  117.8 0.5 collective-permute-start.28
  118.3 3.4 %collective-permute-done.30.refs_6_ = bf16[224,256]{1,0:T(8,128)(2,1)} collective-permute-done((bf16[224,256]{1,0:T(8,128)(2,1)S(1)}, bf16[224,256]{1,0:T(8,128)(2,1)}, u32[]{:S(2)}, u32[]{:S(2)}) %collective-permute-start.30) | collective-permute-done | bytes 114720 | tf_op jit(solution)/shard_map/ppermute | solution.py:50
  121.7 0.5 collective-permute-start.31
  122.3 1.8 %fusion.10 = (bf16[1024,256]{1,0:T(8,128)(2,1)S(1)}, bf16[1024,256]{1,0:T(8,128)(2,1)S(1)}) fusion(bf16[4,1024,256]{2,1,0:T(8,128)(2,1)} %collective-permute-done.17, bf16[4,1024,256]{2,1,0:T(8,128)(2,1)} %copy-done.1), kind=kLoop, calls=%fused_computation.19 | loop fusion | flops 2097152 | bytes 3145728 | tf_op jit(solution)/shard_map/convert_element_type | solution.py:92
  124.0 0.7 collective-permute-start.18
  124.8 1.3 collective-permute-start.19
  126.2 0.7 collective-permute-start.14
  126.9 15.6 %heavy_ffn.1 = (bf16[4,224,256]{2,1,0:T(8,128)(2,1)S(1)}, bf16[4,224,256]{2,1,0:T(8,128)(2,1)S(1)}) custom-call(s32[16]{0:T(128)S(1)} %concatenate.10.offsets, bf16[1,2048]{1,0:T(2,128)(2,1)S(1)} %broadcast_in_dim.20.gain_ref, bf16[2,2048,2560]{2,1,0:T(8,128)(2,1)} %in_ref.1, bf16[2560,2048]{1,0:T(8,128)(2,1)} %down_hbm.1, ...), custom_call_target="tpu_custom_call" | custom-call | flops 14092861440 | bytes 1 | tf_op jit(solution)/shard_map/heavy_ffn/pallas_call | solution.py:361
  142.5 0.1 collective-permute-start.32
  142.6 1.2 fusion
  143.9 0.5 collective-permute-start.20
  144.4 1.4 fusion.4
  145.8 1.6 collective-permute-start.16
  147.4 0.1 fusion.20
  147.5 1.4 collective-permute-start.34
  148.9 0.6 fusion.21.used_ref
  149.5 4.2 %collective-permute-done.34 = bf16[224,256]{1,0:T(8,128)(2,1)S(1)} collective-permute-done((bf16[224,256]{1,0:T(8,128)(2,1)S(1)}, bf16[224,256]{1,0:T(8,128)(2,1)S(1)}, u32[]{:S(2)}, u32[]{:S(2)}) %collective-permute-start.34) | collective-permute-done | bytes 114720 | tf_op jit(solution)/shard_map/ppermute | solution.py:50
  153.6 1.3 collective-permute-start.33
  155.0 0.4 collective-permute-start.35
  155.5 5.7 %collective-permute-done.16 = bf16[1024,256]{1,0:T(8,128)(2,1)S(1)} collective-permute-done((bf16[1024,256]{1,0:T(8,128)(2,1)S(1)}, bf16[1024,256]{1,0:T(8,128)(2,1)S(1)}, u32[]{:S(2)}, u32[]{:S(2)}) %collective-permute-start.16) | collective-permute-done | bytes 524320 | tf_op jit(solution)/shard_map/ppermute | solution.py:50
  161.2 1.8 %fusion.3 = (bf16[1024,256]{1,0:T(8,128)(2,1)S(1)}, bf16[1024,256]{1,0:T(8,128)(2,1)S(1)}) fusion(bf16[1024,256]{1,0:T(8,128)(2,1)S(1)} %collective-permute-done.20, bf16[1024,256]{1,0:T(8,128)(2,1)S(1)} %collective-permute-done.18, bf16[4,1024,256]{2,1,0:T(8,128)(2,1)} %collective-permute-done.17, bf16[4,1024,256]{2,1,0:T(8,128)(2,1)S(1)} %copy-done.2, ...), kind=kLoop, calls=%fused_computation.6 | loop fusion | flops 5242880 | bytes 6291456 | tf_op jit(solution)/shard_map/convert_element_type | solution.py:492
  163.1 1.8 %spread_rows.1 = bf16[2048,256]{1,0:T(8,128)(2,1)} custom-call(s32[1,224]{1,0:T(1,128)S(1)} %copy-done.4, s32[224,1]{1,0:T(8,128)S(1)} %fusion.21.used_ref, bf16[1024,256]{1,0:T(8,128)(2,1)S(1)} %get-tuple-element.38.refs_0_, bf16[1024,256]{1,0:T(8,128)(2,1)S(1)} %get-tuple-element.37.refs_1_, bf16[4,224,256]{2,1,0:T(8,128)(2,1)S(1)} %get-tuple-element.31.refs_2_, ...), custom_call_target="tpu_custom_call" | custom-call | tf_op jit(solution)/shard_map/spread_rows/pallas_call | solution.py:411
  (67 shorter events, 0.3 us)
Async XLA Ops:
  0.0 43.1 %copy-start = (bf16[2048,256]{1,0:T(8,128)(2,1)S(1)}, bf16[2048,256]{1,0:T(8,128)(2,1)}, u32[]{:S(2)}) copy-start(bf16[2048,256]{1,0:T(8,128)(2,1)} %refs_0_.5) | copy-start | bytes 3145732
  0.0 34.3 %copy-start.10 = (bf16[2048]{0:T(1024)(128)(2,1)S(1)}, bf16[2048]{0:T(1024)(128)(2,1)}, u32[]{:S(2)}) copy-start(bf16[2048]{0:T(1024)(128)(2,1)} %param.10) | copy-start | bytes 12292
  0.0 34.3 %copy-start.4 = (s32[1,224]{1,0:T(1,128)S(1)}, s32[1,224]{1,0:T(1,128)}, u32[]{:S(2)}) copy-start(s32[1,224]{1,0:T(1,128)} %rows_ref.1) | copy-start | bytes 2692
  0.0 26.9 %collective-permute-start.1 = (bf16[2048,256]{1,0:T(8,128)(2,1)}, bf16[2048,256]{1,0:T(8,128)(2,1)}, u32[]{:S(2)}, u32[]{:S(2)}) collective-permute-start(bf16[2048,256]{1,0:T(8,128)(2,1)} %refs_0_.5), channel_id=1, source_target_pairs={{0,4},{1,3},{2,6},{3,1},{4,0},{5,7},{6,2},{7,5},{8,12},{9,11},{10,... | collective-permute-start | bytes 3145736 | tf_op jit(solution)/shard_map/ppermute | solution.py:50
  3.0 23.8 %collective-permute-start = (bf16[2048,256]{1,0:T(8,128)(2,1)}, bf16[2048,256]{1,0:T(8,128)(2,1)S(1)}, u32[]{:S(2)}, u32[]{:S(2)}) collective-permute-start(bf16[2048,256]{1,0:T(8,128)(2,1)} %refs_0_.5), channel_id=1, source_target_pairs={{0,2},{1,5},{2,0},{3,7},{4,6},{5,1},{6,4},{7,3},{8,10},{9,13},{10,... | collective-permute-start | bytes 3145736 | tf_op jit(solution)/shard_map/ppermute | solution.py:50
  4.5 26.4 %collective-permute-start.2 = (bf16[2048,256]{1,0:T(8,128)(2,1)}, bf16[2048,256]{1,0:T(8,128)(2,1)S(1)}, u32[]{:S(2)}, u32[]{:S(2)}) collective-permute-start(bf16[2048,256]{1,0:T(8,128)(2,1)} %refs_0_.5), channel_id=1, source_target_pairs={{0,1},{1,0},{2,3},{3,2},{4,5},{5,4},{6,7},{7,6},{8,9},{9,8},{10,11... | collective-permute-start | bytes 3145736 | tf_op jit(solution)/shard_map/ppermute | solution.py:50
  26.9 16.2 %collective-permute-start.4 = (bf16[2048,256]{1,0:T(8,128)(2,1)}, bf16[2048,256]{1,0:T(8,128)(2,1)}, u32[]{:S(2)}, u32[]{:S(2)}) collective-permute-start(bf16[2048,256]{1,0:T(8,128)(2,1)} %collective-permute-done.1.refs_2_), channel_id=1, source_target_pairs={{0,1},{1,0},{2,3},{3,2},{4,5},{5,4},{6,7},{7,6},{8,9},{9,8},{10,11... | collective-permute-start | bytes 3145736 | tf_op jit(solution)/shard_map/ppermute | solution.py:50
  26.9 16.2 %collective-permute-start.3 = (bf16[2048,256]{1,0:T(8,128)(2,1)S(1)}, bf16[2048,256]{1,0:T(8,128)(2,1)}, u32[]{:S(2)}, u32[]{:S(2)}) collective-permute-start(bf16[2048,256]{1,0:T(8,128)(2,1)S(1)} %collective-permute-done.refs_1_), channel_id=1, source_target_pairs={{0,1},{1,0},{2,3},{3,2},{4,5},{5,4},{6,7},{7,6},{8,9},{9,8},{10,11... | collective-permute-start | bytes 3145736 | tf_op jit(solution)/shard_map/ppermute | solution.py:50
  27.4 6.9 %collective-permute-start.5 = (bf16[512,256]{1,0:T(8,128)(2,1)S(1)}, bf16[512,256]{1,0:T(8,128)(2,1)S(1)}, u32[]{:S(2)}, u32[]{:S(2)}) collective-permute-start(bf16[512,256]{1,0:T(8,128)(2,1)S(1)} %pad_maximum_fusion), channel_id=1, source_target_pairs={{0,4},{1,3},{2,6},{3,1},{4,0},{5,7},{6,2},{7,5},{8,12},{9,11},{10,... | collective-permute-start | bytes 786440 | tf_op jit(solution)/shard_map/ppermute | solution.py:50
  30.9 8.1 %collective-permute-start.9 = (bf16[768,256]{1,0:T(8,128)(2,1)}, bf16[768,256]{1,0:T(8,128)(2,1)}, u32[]{:S(2)}, u32[]{:S(2)}) collective-permute-start(bf16[768,256]{1,0:T(8,128)(2,1)} %get-tuple-element.39), channel_id=1, source_target_pairs={{0,4},{1,3},{2,6},{3,1},{4,0},{5,7},{6,2},{7,5},{8,12},{9,11},{10,... | collective-permute-start | bytes 1179656 | tf_op jit(solution)/shard_map/ppermute | solution.py:50
  30.9 1.0 copy-start.7
  31.9 11.2 %collective-permute-start.7 = (bf16[768,256]{1,0:T(8,128)(2,1)}, bf16[768,256]{1,0:T(8,128)(2,1)S(1)}, u32[]{:S(2)}, u32[]{:S(2)}) collective-permute-start(bf16[768,256]{1,0:T(8,128)(2,1)} %get-tuple-element.40), channel_id=1, source_target_pairs={{0,4},{1,3},{2,6},{3,1},{4,0},{5,7},{6,2},{7,5},{8,12},{9,11},{10,... | collective-permute-start | bytes 1179656 | tf_op jit(solution)/shard_map/ppermute | solution.py:50
  34.3 8.8 %collective-permute-start.6 = (bf16[512,256]{1,0:T(8,128)(2,1)S(1)}, bf16[512,256]{1,0:T(8,128)(2,1)}, u32[]{:S(2)}, u32[]{:S(2)}) collective-permute-start(bf16[512,256]{1,0:T(8,128)(2,1)S(1)} %collective-permute-done.5.refs_6_), channel_id=1, source_target_pairs={{0,1},{1,0},{2,3},{3,2},{4,5},{5,4},{6,7},{7,6},{8,9},{9,8},{10,11... | collective-permute-start | bytes 786440 | tf_op jit(solution)/shard_map/ppermute | solution.py:50
  39.0 23.0 %collective-permute-start.10 = (bf16[768,256]{1,0:T(8,128)(2,1)}, bf16[768,256]{1,0:T(8,128)(2,1)S(1)}, u32[]{:S(2)}, u32[]{:S(2)}) collective-permute-start(bf16[768,256]{1,0:T(8,128)(2,1)} %collective-permute-done.9.refs_6_), channel_id=1, source_target_pairs={{0,1},{1,0},{2,3},{3,2},{4,5},{5,4},{6,7},{7,6},{8,9},{9,8},{10,11... | collective-permute-start | bytes 1179656 | tf_op jit(solution)/shard_map/ppermute | solution.py:50
  43.1 13.5 %collective-permute-start.8 = (bf16[768,256]{1,0:T(8,128)(2,1)S(1)}, bf16[768,256]{1,0:T(8,128)(2,1)S(1)}, u32[]{:S(2)}, u32[]{:S(2)}) collective-permute-start(bf16[768,256]{1,0:T(8,128)(2,1)S(1)} %collective-permute-done.7.refs_6_), channel_id=1, source_target_pairs={{0,1},{1,0},{2,3},{3,2},{4,5},{5,4},{6,7},{7,6},{8,9},{9,8},{10,11... | collective-permute-start | bytes 1179656 | tf_op jit(solution)/shard_map/ppermute | solution.py:50
  43.1 1.9 %copy-start.5 = (bf16[3,2048,256]{2,1,0:T(8,128)(2,1)S(1)}, bf16[3,2048,256]{2,1,0:T(8,128)(2,1)}, u32[]{:S(2)}) copy-start(bf16[3,2048,256]{2,1,0:T(8,128)(2,1)} %weight_ref.8) | copy-start | bytes 9437188
  45.0 1.2 copy-start.8
  50.5 17.0 %collective-permute-start.12 = (bf16[128,512]{1,0:T(8,128)(2,1)S(1)}, bf16[128,512]{1,0:T(8,128)(2,1)S(1)}, u32[]{:S(2)}, u32[]{:S(2)}) collective-permute-start(bf16[128,512]{1,0:T(8,128)(2,1)S(1)} %get-tuple-element.47), channel_id=1, source_target_pairs={{8,0},{16,8},{24,16},{9,1},{17,9},{25,17},{10,2},{18,10},{26,18},{... | collective-permute-start | bytes 393224 | tf_op jit(solution)/shard_map/ppermute | solution.py:468
  51.8 15.7 %collective-permute-start.11 = (bf16[128,512]{1,0:T(8,128)(2,1)S(1)}, bf16[128,512]{1,0:T(8,128)(2,1)S(1)}, u32[]{:S(2)}, u32[]{:S(2)}) collective-permute-start(bf16[128,512]{1,0:T(8,128)(2,1)S(1)} %get-tuple-element.48), channel_id=1, source_target_pairs={{0,8},{8,16},{16,24},{1,9},{9,17},{17,25},{2,10},{10,18},{18,26},{... | collective-permute-start | bytes 393224 | tf_op jit(solution)/shard_map/ppermute | solution.py:467
  61.9 5.6 %copy-start.6 = (bf16[256,2048]{1,0:T(8,128)(2,1)S(1)}, bf16[256,2048]{1,0:T(8,128)(2,1)}, u32[]{:S(2)}) copy-start(bf16[256,2048]{1,0:T(8,128)(2,1)} %weight_ref.11) | copy-start | bytes 3145732
  75.2 6.1 %copy-start.3 = (bf16[4,224,256]{2,1,0:T(8,128)(2,1)}, bf16[4,224,256]{2,1,0:T(8,128)(2,1)S(1)}, u32[]{:S(2)}) copy-start(bf16[4,224,256]{2,1,0:T(8,128)(2,1)S(1)} %get-tuple-element.25.refs_8_) | copy-start | bytes 1376260
  81.3 21.3 %collective-permute-start.13 = (bf16[4,1024,256]{2,1,0:T(8,128)(2,1)}, bf16[4,1024,256]{2,1,0:T(8,128)(2,1)}, u32[]{:S(2)}, u32[]{:S(2)}) collective-permute-start(bf16[4,1024,256]{2,1,0:T(8,128)(2,1)} %get-tuple-element.27), channel_id=1, source_target_pairs={{0,1},{1,0},{2,3},{3,2},{4,5},{5,4},{6,7},{7,6},{8,9},{9,8},{10,11... | collective-permute-start | bytes 6291464 | tf_op jit(solution)/shard_map/ppermute | solution.py:50
  87.2 1.4 copy-start.1
  88.5 33.2 %collective-permute-start.17 = (bf16[4,1024,256]{2,1,0:T(8,128)(2,1)}, bf16[4,1024,256]{2,1,0:T(8,128)(2,1)}, u32[]{:S(2)}, u32[]{:S(2)}) collective-permute-start(bf16[4,1024,256]{2,1,0:T(8,128)(2,1)} %get-tuple-element.29), channel_id=1, source_target_pairs={{0,1},{1,0},{2,3},{3,2},{4,5},{5,4},{6,7},{7,6},{8,9},{9,8},{10,11... | collective-permute-start | bytes 6291464 | tf_op jit(solution)/shard_map/ppermute | solution.py:50
  89.1 4.8 %collective-permute-start.21 = (bf16[4,224,256]{2,1,0:T(8,128)(2,1)}, bf16[4,224,256]{2,1,0:T(8,128)(2,1)}, u32[]{:S(2)}, u32[]{:S(2)}) collective-permute-start(bf16[4,224,256]{2,1,0:T(8,128)(2,1)} %get-tuple-element.30), channel_id=1, source_target_pairs={{0,1},{1,0},{2,3},{3,2},{4,5},{5,4},{6,7},{7,6},{8,9},{9,8},{10,11... | collective-permute-start | bytes 1376264 | tf_op jit(solution)/shard_map/ppermute | solution.py:50
  95.0 4.9 %collective-permute-start.23 = (bf16[224,256]{1,0:T(8,128)(2,1)S(1)}, bf16[224,256]{1,0:T(8,128)(2,1)S(1)}, u32[]{:S(2)}, u32[]{:S(2)}) collective-permute-start(bf16[224,256]{1,0:T(8,128)(2,1)S(1)} %get-tuple-element.46), channel_id=1, source_target_pairs={{0,2},{1,5},{2,0},{3,7},{4,6},{5,1},{6,4},{7,3},{8,10},{9,13},{10,... | collective-permute-start | bytes 344072 | tf_op jit(solution)/shard_map/ppermute | solution.py:50
  95.7 21.5 %copy-start.11 = (bf16[2048]{0:T(1024)(128)(2,1)S(1)}, bf16[2048]{0:T(1024)(128)(2,1)}, u32[]{:S(2)}) copy-start(bf16[2048]{0:T(1024)(128)(2,1)} %param.13) | copy-start | bytes 12292
  95.7 21.5 %copy-start.12 = (s32[4]{0:T(128)S(1)}, s32[4]{0:T(128)}, u32[]{:S(2)}) copy-start(s32[4]{0:T(128)} %param.17) | copy-start | bytes 52
  95.7 9.9 %collective-permute-start.22 = (bf16[224,256]{1,0:T(8,128)(2,1)S(1)}, bf16[224,256]{1,0:T(8,128)(2,1)S(1)}, u32[]{:S(2)}, u32[]{:S(2)}) collective-permute-start(bf16[224,256]{1,0:T(8,128)(2,1)S(1)} %get-tuple-element.45), channel_id=1, source_target_pairs={{0,2},{1,5},{2,0},{3,7},{4,6},{5,1},{6,4},{7,3},{8,10},{9,13},{10,... | collective-permute-start | bytes 344072 | tf_op jit(solution)/shard_map/ppermute | solution.py:50
  100.8 4.9 %collective-permute-start.24 = (bf16[224,256]{1,0:T(8,128)(2,1)S(1)}, bf16[224,256]{1,0:T(8,128)(2,1)S(1)}, u32[]{:S(2)}, u32[]{:S(2)}) collective-permute-start(bf16[224,256]{1,0:T(8,128)(2,1)S(1)} %fusion.13), channel_id=1, source_target_pairs={{0,4},{1,3},{2,6},{3,1},{4,0},{5,7},{6,2},{7,5},{8,12},{9,11},{10,... | collective-permute-start | bytes 344072 | tf_op jit(solution)/shard_map/ppermute | solution.py:50
  105.0 21.9 %collective-permute-start.15 = (bf16[1024,256]{1,0:T(8,128)(2,1)}, bf16[1024,256]{1,0:T(8,128)(2,1)}, u32[]{:S(2)}, u32[]{:S(2)}) collective-permute-start(bf16[1024,256]{1,0:T(8,128)(2,1)} %get-tuple-element.36), channel_id=1, source_target_pairs={{0,2},{1,5},{2,0},{3,7},{4,6},{5,1},{6,4},{7,3},{8,10},{9,13},{10,... | collective-permute-start | bytes 1572872 | tf_op jit(solution)/shard_map/ppermute | solution.py:50
  106.7 10.1 %collective-permute-start.25 = (bf16[224,256]{1,0:T(8,128)(2,1)S(1)}, bf16[224,256]{1,0:T(8,128)(2,1)S(1)}, u32[]{:S(2)}, u32[]{:S(2)}) collective-permute-start(bf16[224,256]{1,0:T(8,128)(2,1)S(1)} %fusion.16.refs_0_), channel_id=1, source_target_pairs={{0,2},{1,5},{2,0},{3,7},{4,6},{5,1},{6,4},{7,3},{8,10},{9,13},{10,... | collective-permute-start | bytes 344072 | tf_op jit(solution)/shard_map/ppermute | solution.py:50
  108.2 9.7 %collective-permute-start.26 = (bf16[224,256]{1,0:T(8,128)(2,1)S(1)}, bf16[224,256]{1,0:T(8,128)(2,1)S(1)}, u32[]{:S(2)}, u32[]{:S(2)}) collective-permute-start(bf16[224,256]{1,0:T(8,128)(2,1)S(1)} %fusion.16.refs_0_), channel_id=1, source_target_pairs={{0,4},{1,3},{2,6},{3,1},{4,0},{5,7},{6,2},{7,5},{8,12},{9,11},{10,... | collective-permute-start | bytes 344072 | tf_op jit(solution)/shard_map/ppermute | solution.py:50
  116.8 4.9 %collective-permute-start.30 = (bf16[224,256]{1,0:T(8,128)(2,1)S(1)}, bf16[224,256]{1,0:T(8,128)(2,1)}, u32[]{:S(2)}, u32[]{:S(2)}) collective-permute-start(bf16[224,256]{1,0:T(8,128)(2,1)S(1)} %collective-permute-done.25.refs_1_), channel_id=1, source_target_pairs={{0,4},{1,3},{2,6},{3,1},{4,0},{5,7},{6,2},{7,5},{8,12},{9,11},{10,... | collective-permute-start | bytes 344072 | tf_op jit(solution)/shard_map/ppermute | solution.py:50
  117.2 8.9 %copy-start.9 = (bf16[1024,256]{1,0:T(8,128)(2,1)S(1)}, bf16[1024,256]{1,0:T(8,128)(2,1)}, u32[]{:S(2)}) copy-start(bf16[1024,256]{1,0:T(8,128)(2,1)} %get-tuple-element.35) | copy-start | bytes 1572868
  117.8 6.2 %collective-permute-start.27 = (bf16[224,256]{1,0:T(8,128)(2,1)S(1)}, bf16[224,256]{1,0:T(8,128)(2,1)S(1)}, u32[]{:S(2)}, u32[]{:S(2)}) collective-permute-start(bf16[224,256]{1,0:T(8,128)(2,1)S(1)} %fusion.16.refs_0_), channel_id=1, source_target_pairs={{0,1},{1,0},{2,3},{3,2},{4,5},{5,4},{6,7},{7,6},{8,9},{9,8},{10,11... | collective-permute-start | bytes 344072 | tf_op jit(solution)/shard_map/ppermute | solution.py:50
  117.8 8.3 %collective-permute-start.28 = (bf16[224,256]{1,0:T(8,128)(2,1)S(1)}, bf16[224,256]{1,0:T(8,128)(2,1)S(1)}, u32[]{:S(2)}, u32[]{:S(2)}) collective-permute-start(bf16[224,256]{1,0:T(8,128)(2,1)S(1)} %collective-permute-done.25.refs_1_), channel_id=1, source_target_pairs={{0,1},{1,0},{2,3},{3,2},{4,5},{5,4},{6,7},{7,6},{8,9},{9,8},{10,11... | collective-permute-start | bytes 344072 | tf_op jit(solution)/shard_map/ppermute | solution.py:50
  121.7 3.1 %collective-permute-start.29 = (bf16[224,256]{1,0:T(8,128)(2,1)S(1)}, bf16[224,256]{1,0:T(8,128)(2,1)S(1)}, u32[]{:S(2)}, u32[]{:S(2)}) collective-permute-start(bf16[224,256]{1,0:T(8,128)(2,1)S(1)} %collective-permute-done.26.refs_2_), channel_id=1, source_target_pairs={{0,1},{1,0},{2,3},{3,2},{4,5},{5,4},{6,7},{7,6},{8,9},{9,8},{10,11... | collective-permute-start | bytes 344072 | tf_op jit(solution)/shard_map/ppermute | solution.py:50
  121.7 5.1 %collective-permute-start.31 = (bf16[224,256]{1,0:T(8,128)(2,1)}, bf16[224,256]{1,0:T(8,128)(2,1)S(1)}, u32[]{:S(2)}, u32[]{:S(2)}) collective-permute-start(bf16[224,256]{1,0:T(8,128)(2,1)} %collective-permute-done.30.refs_6_), channel_id=1, source_target_pairs={{0,1},{1,0},{2,3},{3,2},{4,5},{5,4},{6,7},{7,6},{8,9},{9,8},{10,11... | collective-permute-start | bytes 344072 | tf_op jit(solution)/shard_map/ppermute | solution.py:50
  124.0 31.0 %collective-permute-start.18 = (bf16[1024,256]{1,0:T(8,128)(2,1)S(1)}, bf16[1024,256]{1,0:T(8,128)(2,1)S(1)}, u32[]{:S(2)}, u32[]{:S(2)}) collective-permute-start(bf16[1024,256]{1,0:T(8,128)(2,1)S(1)} %get-tuple-element.33), channel_id=1, source_target_pairs={{0,2},{1,5},{2,0},{3,7},{4,6},{5,1},{6,4},{7,3},{8,10},{9,13},{10,... | collective-permute-start | bytes 1572872 | tf_op jit(solution)/shard_map/ppermute | solution.py:50
  124.8 17.8 %collective-permute-start.19 = (bf16[1024,256]{1,0:T(8,128)(2,1)S(1)}, bf16[1024,256]{1,0:T(8,128)(2,1)S(1)}, u32[]{:S(2)}, u32[]{:S(2)}) collective-permute-start(bf16[1024,256]{1,0:T(8,128)(2,1)S(1)} %get-tuple-element.34), channel_id=1, source_target_pairs={{0,2},{1,5},{2,0},{3,7},{4,6},{5,1},{6,4},{7,3},{8,10},{9,13},{10,... | collective-permute-start | bytes 1572872 | tf_op jit(solution)/shard_map/ppermute | solution.py:50
  126.1 16.5 %copy-start.2 = (bf16[4,1024,256]{2,1,0:T(8,128)(2,1)S(1)}, bf16[4,1024,256]{2,1,0:T(8,128)(2,1)}, u32[]{:S(2)}) copy-start(bf16[4,1024,256]{2,1,0:T(8,128)(2,1)} %copy-done.1) | copy-start | bytes 6291460
  126.2 29.3 %collective-permute-start.14 = (bf16[1024,256]{1,0:T(8,128)(2,1)S(1)}, bf16[1024,256]{1,0:T(8,128)(2,1)S(1)}, u32[]{:S(2)}, u32[]{:S(2)}) collective-permute-start(bf16[1024,256]{1,0:T(8,128)(2,1)S(1)} %copy-done.9), channel_id=1, source_target_pairs={{0,2},{1,5},{2,0},{3,7},{4,6},{5,1},{6,4},{7,3},{8,10},{9,13},{10,... | collective-permute-start | bytes 1572872 | tf_op jit(solution)/shard_map/ppermute | solution.py:50
  142.5 4.9 %collective-permute-start.32 = (bf16[4,224,256]{2,1,0:T(8,128)(2,1)S(1)}, bf16[4,224,256]{2,1,0:T(8,128)(2,1)S(1)}, u32[]{:S(2)}, u32[]{:S(2)}) collective-permute-start(bf16[4,224,256]{2,1,0:T(8,128)(2,1)S(1)} %get-tuple-element.32), channel_id=1, source_target_pairs={{0,1},{1,0},{2,3},{3,2},{4,5},{5,4},{6,7},{7,6},{8,9},{9,8},{10,11... | collective-permute-start | bytes 1376264 | tf_op jit(solution)/shard_map/ppermute | solution.py:50
  143.9 11.6 %collective-permute-start.20 = (bf16[1024,256]{1,0:T(8,128)(2,1)S(1)}, bf16[1024,256]{1,0:T(8,128)(2,1)S(1)}, u32[]{:S(2)}, u32[]{:S(2)}) collective-permute-start(bf16[1024,256]{1,0:T(8,128)(2,1)S(1)} %fusion), channel_id=1, source_target_pairs={{0,4},{1,3},{2,6},{3,1},{4,0},{5,7},{6,2},{7,5},{8,12},{9,11},{10,... | collective-permute-start | bytes 1572872 | tf_op jit(solution)/shard_map/ppermute | solution.py:50
  145.8 15.4 %collective-permute-start.16 = (bf16[1024,256]{1,0:T(8,128)(2,1)S(1)}, bf16[1024,256]{1,0:T(8,128)(2,1)S(1)}, u32[]{:S(2)}, u32[]{:S(2)}) collective-permute-start(bf16[1024,256]{1,0:T(8,128)(2,1)S(1)} %fusion.4), channel_id=1, source_target_pairs={{0,4},{1,3},{2,6},{3,1},{4,0},{5,7},{6,2},{7,5},{8,12},{9,11},{10,... | collective-permute-start | bytes 1572872 | tf_op jit(solution)/shard_map/ppermute | solution.py:50
  147.5 6.2 %collective-permute-start.34 = (bf16[224,256]{1,0:T(8,128)(2,1)S(1)}, bf16[224,256]{1,0:T(8,128)(2,1)S(1)}, u32[]{:S(2)}, u32[]{:S(2)}) collective-permute-start(bf16[224,256]{1,0:T(8,128)(2,1)S(1)} %get-tuple-element.43), channel_id=1, source_target_pairs={{0,2},{1,5},{2,0},{3,7},{4,6},{5,1},{6,4},{7,3},{8,10},{9,13},{10,... | collective-permute-start | bytes 344072 | tf_op jit(solution)/shard_map/ppermute | solution.py:50
  153.6 9.4 %collective-permute-start.33 = (bf16[224,256]{1,0:T(8,128)(2,1)S(1)}, bf16[224,256]{1,0:T(8,128)(2,1)S(1)}, u32[]{:S(2)}, u32[]{:S(2)}) collective-permute-start(bf16[224,256]{1,0:T(8,128)(2,1)S(1)} %get-tuple-element.44), channel_id=1, source_target_pairs={{0,2},{1,5},{2,0},{3,7},{4,6},{5,1},{6,4},{7,3},{8,10},{9,13},{10,... | collective-permute-start | bytes 344072 | tf_op jit(solution)/shard_map/ppermute | solution.py:50
  155.0 8.0 %collective-permute-start.35 = (bf16[224,256]{1,0:T(8,128)(2,1)S(1)}, bf16[224,256]{1,0:T(8,128)(2,1)S(1)}, u32[]{:S(2)}, u32[]{:S(2)}) collective-permute-start(bf16[224,256]{1,0:T(8,128)(2,1)S(1)} %fusion.12), channel_id=1, source_target_pairs={{0,4},{1,3},{2,6},{3,1},{4,0},{5,7},{6,2},{7,5},{8,12},{9,11},{10,... | collective-permute-start | bytes 344072 | tf_op jit(solution)/shard_map/ppermute | solution.py:50
